TPU v7x, 128 devices: a whole 4x4x4 slice. The times are simulated.
128 devices in a mesh: row: 8 (over y_lo, z), col: 16 (over x, y_hi, core).
Axes of the slice: x: 4, y: 4 (y_hi: 2, y_lo: 2; y = y_hi * 2 + y_lo), z: 4, core: 2. Of those that a mesh axis runs over, the one named last changes fastest.
Arguments:
- tokens: bfloat16 [1024, 12288], P('col', 'row'), may hold values from -6 to 6
- widen_blocks: bfloat16 [8, 576, 128, 128], P('row', 'col'), may hold values from -0.125 to 0.125
- widen_pattern: int32 [8, 576, 2], P('row', 'col'), may hold values from -1 to 11, as said below
- narrow_blocks: bfloat16 [8, 576, 128, 128], P('row', 'col'), may hold values from -0.078125 to 0.078125
- narrow_pattern: int32 [8, 576, 2], P('row', 'col'), may hold values from -1 to 11, as said below
- cotangent: bfloat16 [1024, 12288], P('col', 'row'), may hold values from -6 to 6
Outputs:
- layer_output: bfloat16 [1024, 12288], P('col', 'row')
- token_grad: bfloat16 [1024, 12288], P('col', 'row')
- widen_grad: bfloat16 [8, 576, 128, 128], P('row', 'col')
- narrow_grad: bfloat16 [8, 576, 128, 128], P('row', 'col')
Inputs may be any that keep to these rules, and one draw needn't show every extreme that they name: `widen_pattern`: in each tile the live slots come first and name distinct blocks with entries (r, c), r below 12 and c below 12; the other slots hold -1 in both entries; some tile has all 36 slots live. `narrow_pattern`: in each tile the live slots come first and name distinct blocks with entries (r, c), r below 12 and c below 12; the other slots hold -1 in both entries; some tile has all 36 slots live.
All inputs are finite; a program needn't handle non-finite values.
Results may differ from a plain program's by a relative error of at most 0.028.
Values may be sent and summed in bfloat16 or wider, within the bound.
A program may use at most 128 MiB of HBM per device.

v0:
```python
import math

import jax
import jax.numpy as jnp
from jax import lax
from jax.sharding import PartitionSpec as P

FF = 24576


def gelu_back(pre_value, upstream):
    return jax.vjp(jax.nn.gelu, pre_value)[1](upstream)[0]


def dense_tile(values, in_index, out_index, in_count, out_count):
    side = values.shape[-1]
    is_live = in_index >= 0
    flat_index = jnp.maximum(in_index, 0) * out_count + jnp.maximum(out_index, 0)
    selector = (
        flat_index[:, None] == jnp.arange(in_count * out_count, dtype=jnp.int32)[None, :]
    ) & is_live[:, None]
    placed = jnp.einsum(
        "cn,crk->nrk", selector.astype(values.dtype), values, preferred_element_type=jnp.float32
    )
    placed = placed.astype(jnp.bfloat16).reshape(in_count, out_count, side, side)
    return placed.transpose(0, 2, 1, 3).reshape(in_count * side, out_count * side)


def times_tile(source, tile_matrix):
    return jnp.dot(source, tile_matrix, preferred_element_type=jnp.float32)


def times_flipped(source, tile_matrix):
    return lax.dot_general(
        source, tile_matrix, (((1,), (1,)), ((), ())), preferred_element_type=jnp.float32
    )


def pick_blocks(source, choose, number):
    height = source.shape[0]
    grouped = source.reshape(height, number, source.shape[1] // number)
    return jnp.take(grouped, jnp.maximum(choose, 0), axis=1)


def slot_grads(left, right, left_index, right_index, left_count, right_count, factor):
    left_picked = pick_blocks(left, left_index, left_count)
    right_picked = pick_blocks(right, right_index, right_count)
    summed = jnp.einsum(
        "tcr,tck->crk", left_picked, right_picked, preferred_element_type=jnp.float32
    )
    is_live = left_index >= 0
    return jnp.where(is_live[:, None, None], summed * factor, 0.0).astype(jnp.bfloat16)


def local(tokens, widen_blocks, widen_pattern, narrow_blocks, narrow_pattern, cotangent):
    block_side = widen_blocks.shape[-1]
    model_blocks = tokens.shape[1] // block_side
    hidden_blocks = FF // (lax.axis_size("col") * block_side)
    widen_inputs = widen_pattern[0, :, 0]
    widen_outputs = widen_pattern[0, :, 1]
    narrow_inputs = narrow_pattern[0, :, 0]
    narrow_outputs = narrow_pattern[0, :, 1]
    widen_tile = dense_tile(
        widen_blocks[0], widen_inputs, widen_outputs, model_blocks, hidden_blocks
    )
    narrow_tile = dense_tile(
        narrow_blocks[0], narrow_inputs, narrow_outputs, hidden_blocks, model_blocks
    )
    all_tokens, all_cotangent = (
        lax.all_gather(tokens, "col", axis=0, tiled=True),
        lax.all_gather(cotangent, "col", axis=0, tiled=True),
    )
    height = all_tokens.shape[0]
    row_share = height // lax.axis_size("row")
    col_share = tokens.shape[0]
    factor = 1.0 / math.sqrt(height)

    def widen_term(first_row, length):
        return times_tile(all_tokens, widen_tile)

    def narrow_back_term(first_row, length):
        return times_flipped(all_cotangent, narrow_tile)

    def row_sum(action):
        return lax.psum_scatter(
            action(jnp.int32(0), row_share * lax.axis_size("row")).astype(jnp.bfloat16),
            "row",
            scatter_dimension=0,
            tiled=True,
        ).astype(jnp.float32)

    def row_collect(field_part):
        return lax.all_gather(field_part, "row", axis=0, tiled=True)

    hidden = row_sum(widen_term)
    activation = row_collect(jax.nn.gelu(hidden).astype(jnp.bfloat16))
    hidden_grad = row_sum(narrow_back_term)
    pre_grad = row_collect(gelu_back(hidden, hidden_grad).astype(jnp.bfloat16))

    def col_sum(action):
        return lax.psum_scatter(
            action(jnp.int32(0), col_share * lax.axis_size("col")).astype(jnp.bfloat16),
            "col",
            scatter_dimension=0,
            tiled=True,
        ).astype(jnp.float32)

    def narrow_term(first_row, length):
        return times_tile(activation, narrow_tile)

    def token_term(first_row, length):
        return times_flipped(pre_grad, widen_tile)

    layer_output = col_sum(narrow_term).astype(jnp.bfloat16)
    token_grad = col_sum(token_term).astype(jnp.bfloat16)
    widen_grad = slot_grads(
        all_tokens, pre_grad, widen_inputs, widen_outputs, model_blocks, hidden_blocks, factor
    )
    narrow_grad = slot_grads(
        activation,
        all_cotangent,
        narrow_inputs,
        narrow_outputs,
        hidden_blocks,
        model_blocks,
        factor,
    )
    return (layer_output, token_grad, widen_grad[None], narrow_grad[None])


def solution(mesh):
    placed = (
        P("col", "row"),
        P("row", "col", None, None),
        P("row", "col", None),
        P("row", "col", None, None),
        P("row", "col", None),
        P("col", "row"),
    )
    return jax.shard_map(
        local,
        mesh=mesh,
        in_specs=placed,
        out_specs=(
            P("col", "row"),
            P("col", "row"),
            P("row", "col", None, None),
            P("row", "col", None, None),
        ),
        check_vma=False,
    )
```

profile of v0, /device:TPU:0, one launch (start us, length us, event | category | flops | bytes accessed | tf_op | source)
XLA Modules:
  0.0 491.9 jit_solution(12878648804327261624)
XLA Ops:
  13.0 6.4 %copy.40 = bf16[12,128,12,128]{3,2,1,0:T(8,128)(2,1)} copy(bf16[12,128,12,128]{3,1,2,0:T(8,128)(2,1)S(1)} %bitcast.112) | data formatting | bytes 9437184 | tf_op jit(solution)/shard_map/transpose | solution.py:26
  19.4 45.8 %all-gather.9.cloned.1.call-done = bf16[1024,1536]{1,0:T(8,128)(2,1)} async-done(((bf16[64,1536]{1,0:T(8,128)(2,1)}), bf16[1024,1536]{1,0:T(8,128)(2,1)}) %all-gather.9.cloned.1.call-update) | async-done | bytes 3145744 | tf_op jit(solution)/shard_map/all_gather | solution.py:71
  65.2 8.6 %fusion.41 = bf16[1024,1536]{0,1:T(8,128)(2,1)S(1)} fusion(bf16[1024,1536]{1,0:T(8,128)(2,1)} %all-gather.9.cloned.1.call-done, bf16[192,8,12,128]{3,2,1,0:T(8,128)(2,1)} %bitcast.116), kind=kOutput, calls=%fused_computation.37 | convolution fusion | flops 4833411072 | bytes 11010048 | tf_op jit(solution)/shard_map/dot_general | solution.py:34
  81.1 6.3 %copy.37 = bf16[12,128,12,128]{3,2,1,0:T(8,128)(2,1)} copy(bf16[12,128,12,128]{3,1,2,0:T(8,128)(2,1)S(1)} %bitcast.113) | data formatting | bytes 9437184 | tf_op jit(solution)/shard_map/transpose | solution.py:26
  87.5 31.1 %all-gather.5.cloned.1.call-done = bf16[1024,1536]{1,0:T(8,128)(2,1)} async-done(((bf16[64,1536]{1,0:T(8,128)(2,1)}), bf16[1024,1536]{1,0:T(8,128)(2,1)}) %all-gather.5.cloned.1.call-update) | async-done | bytes 3145744 | tf_op jit(solution)/shard_map/all_gather | solution.py:70
  118.6 9.4 %fusion.44 = bf16[1024,1536]{0,1:T(8,128)(2,1)S(1)} fusion(bf16[1024,1536]{1,0:T(8,128)(2,1)} %all-gather.5.cloned.1.call-done, bf16[192,8,12,128]{3,2,1,0:T(8,128)(2,1)} %bitcast.118), kind=kOutput, calls=%fused_computation.38 | convolution fusion | flops 4833411072 | bytes 11010048 | tf_op jit(solution)/shard_map/dot_general | solution.py:30
  128.1 3.0 copy.48
  131.2 34.8 %reduce-scatter.15.cloned.1.call-done = bf16[128,1536]{1,0:T(8,128)(2,1)} async-done(((bf16[1024,1536]{1,0:T(8,128)(2,1)}), bf16[128,1536]{1,0:T(8,128)(2,1)}) %reduce-scatter.15.cloned.1.call-update) | async-done | bytes 393232
  167.2 46.7 %reduce-scatter.13.cloned.1.call-done = bf16[128,1536]{1,0:T(8,128)(2,1)} async-done(((bf16[1024,1536]{1,0:T(8,128)(2,1)}), bf16[128,1536]{1,0:T(8,128)(2,1)}) %reduce-scatter.13.cloned.1.call-update) | async-done | bytes 393232
  217.5 51.5 %all-gather.7.cloned.1.call-done = bf16[1024,1536]{0,1:T(8,128)(2,1)} async-done(((bf16[128,1536]{0,1:T(8,128)(2,1)}), bf16[1024,1536]{0,1:T(8,128)(2,1)}) %all-gather.7.cloned.1.call-update) | async-done | bytes 3145744 | tf_op jit(solution)/shard_map/all_gather | solution.py:93
  269.0 9.8 %fusion.31 = bf16[1024,1536]{1,0:T(8,128)(2,1)} fusion(bf16[1024,1536]{0,1:T(8,128)(2,1)} %all-gather.7.cloned.1.call-done, bf16[192,8,12,128]{3,2,1,0:T(8,128)(2,1)} %bitcast.117), kind=kOutput, calls=%fused_computation.31 | convolution fusion | flops 4833411072 | bytes 11010048 | tf_op jit(solution)/shard_map/dot_general | solution.py:30
  278.9 45.8 %all-gather.11.cloned.1.call-done = bf16[1024,1536]{0,1:T(8,128)(2,1)} async-done(((bf16[128,1536]{0,1:T(8,128)(2,1)}), bf16[1024,1536]{0,1:T(8,128)(2,1)}) %all-gather.11.cloned.1.call-update) | async-done | bytes 3145744 | tf_op jit(solution)/shard_map/all_gather | solution.py:93
  324.7 9.6 %fusion.28 = bf16[1024,1536]{1,0:T(8,128)(2,1)} fusion(bf16[1024,1536]{0,1:T(8,128)(2,1)} %all-gather.11.cloned.1.call-done, bf16[192,8,12,128]{3,2,1,0:T(8,128)(2,1)} %bitcast.119), kind=kOutput, calls=%fused_computation.30 | convolution fusion | flops 4833411072 | bytes 11010048 | tf_op jit(solution)/shard_map/dot_general | solution.py:34
  339.1 3.5 copy.42
  342.6 4.7 copy.45
  347.3 4.8 copy.46
  352.1 5.4 %gather_fusion = bf16[36,1024,128]{2,1,0:T(8,128)(2,1)} fusion(bf16[1024,12,128]{2,0,1:T(8,128)(2,1)S(1)} %copy.42, s32[1024]{0:T(1024)S(1)} %get-tuple-element.20), kind=kCustom, calls=%fused_computation.clone | custom fusion | bytes 18874512 | tf_op jit(solution)/shard_map/jit(_take)/gather | solution.py:42
  357.5 7.3 %gather_fusion.3 = bf16[36,1024,128]{2,1,0:T(8,128)(2,1)} fusion(bf16[1024,12,128]{2,0,1:T(8,128)(2,1)} %copy.46, s32[1024]{0:T(1024)S(1)} %get-tuple-element.21), kind=kCustom, calls=%fused_computation.3.clone | custom fusion | bytes 18874512 | tf_op jit(solution)/shard_map/jit(_take)/gather | solution.py:42
  364.8 3.5 copy.43
  368.3 5.5 %gather_fusion.1 = bf16[36,1024,128]{2,1,0:T(8,128)(2,1)} fusion(bf16[1024,12,128]{2,0,1:T(8,128)(2,1)S(1)} %copy.43, s32[1024]{0:T(1024)S(1)} %get-tuple-element.19), kind=kCustom, calls=%fused_computation.1.clone | custom fusion | bytes 18874512 | tf_op jit(solution)/shard_map/jit(_take)/gather | solution.py:42
  373.8 7.6 %gather_fusion.2 = bf16[36,1024,128]{1,2,0:T(8,128)(2,1)} fusion(bf16[1024,12,128]{0,2,1:T(8,128)(2,1)} %bitcast.111, s32[1024]{0:T(1024)S(1)} %get-tuple-element.22), kind=kCustom, calls=%fused_computation.2.clone | custom fusion | bytes 18874512 | tf_op jit(solution)/shard_map/jit(_take)/gather | solution.py:42
  381.4 11.2 %fusion.55 = bf16[1,36,128,128]{3,2,1,0:T(8,128)(2,1)} fusion(bf16[36,1024,128]{2,1,0:T(8,128)(2,1)} %gather_fusion.1, pred[36]{0:T(512)(128)(4,1)S(1)} %get-tuple-element.17, bf16[36,1024,128]{2,1,0:T(8,128)(2,1)} %gather_fusion, pred[36]{0:T(512)(128)(4,1)S(1)} %get-tuple-element.9, pred[36]{0:T(512)(128)(4,1)S(1)} %compare_bitcast_fusion.1), kind=kOutput, calls=%fused_computation.48 | convolution fusion | flops 1219166208 | bytes 20054124 | tf_op jit(solution)/shard_map/tcr,tck->crk/dot_general | solution.py:48
  392.6 10.3 %fusion.60 = bf16[1,36,128,128]{3,2,1,0:T(8,128)(2,1)} fusion(bf16[36,1024,128]{2,1,0:T(8,128)(2,1)} %gather_fusion.3, pred[36]{0:T(512)(128)(4,1)S(1)} %get-tuple-element.15, bf16[36,1024,128]{1,2,0:T(8,128)(2,1)} %gather_fusion.2, pred[36]{0:T(512)(128)(4,1)S(1)} %get-tuple-element.5, pred[36]{0:T(512)(128)(4,1)S(1)} %compare_bitcast_fusion), kind=kOutput, calls=%fused_computation.49 | convolution fusion | flops 1219166208 | bytes 20054124 | tf_op jit(solution)/shard_map/tcr,tck->crk/dot_general | solution.py:48
  406.0 78.7 %reduce-scatter.11.cloned.1.call-done = bf16[64,1536]{1,0:T(8,128)(2,1)} async-done(((bf16[1024,1536]{1,0:T(8,128)(2,1)}), bf16[64,1536]{1,0:T(8,128)(2,1)}) %reduce-scatter.11.cloned.1.call-update) | async-done | bytes 196624 | tf_op jit(solution)/shard_map/reduce_scatter | solution.py:101
  (44 shorter events, 25.7 us)
Async XLA Ops:
  7.2 3.0 copy-start
  7.2 58.0 %all-gather.9.cloned.1.call-start = ((), (), s32[]{:S(2)}) async-start(), calls=%async_computation.7 | async-start | bytes 3342336 | tf_op jit(solution)/shard_map/all_gather | solution.py:71
  7.9 110.7 %all-gather.5.cloned.1.call-start = ((), (), s32[]{:S(2)}) async-start(), calls=%async_computation.4 | async-start | bytes 3342336 | tf_op jit(solution)/shard_map/all_gather | solution.py:70
  8.7 157.3 %reduce-scatter.15.cloned.1.call-start = ((), (), s32[]{:S(2)}) async-start(), calls=%async_computation.11 | async-start | bytes 3538944
  73.8 3.2 copy-start.3
  76.8 137.1 %reduce-scatter.13.cloned.1.call-start = ((), (), s32[]{:S(2)}) async-start(), calls=%async_computation.10 | async-start | bytes 3538944
  131.1 137.9 %all-gather.7.cloned.1.call-start = ((), (), s32[]{:S(2)}) async-start(), calls=%async_computation.5 | async-start | bytes 3538944 | tf_op jit(solution)/shard_map/all_gather | solution.py:93
  216.6 108.1 %all-gather.11.cloned.1.call-start = ((), (), s32[]{:S(2)}) async-start(), calls=%async_computation.8 | async-start | bytes 3538944 | tf_op jit(solution)/shard_map/all_gather | solution.py:93
  217.2 188.7 %reduce-scatter.9.cloned.1.call-start = ((), (), s32[]{:S(2)}) async-start(), calls=%async_computation.6 | async-start | bytes 3342336 | tf_op jit(solution)/shard_map/reduce_scatter | solution.py:101
  278.8 55.5 %copy-start.4 = (s32[1,36,2]{1,2,0:T(2,128)S(1)}, s32[1,36,2]{1,2,0:T(2,128)}, u32[]{:S(2)}) copy-start(s32[1,36,2]{1,2,0:T(2,128)} %param.12) | copy-start | bytes 868
  278.8 205.8 %reduce-scatter.11.cloned.1.call-start = ((), (), s32[]{:S(2)}) async-start(), calls=%async_computation.9 | async-start | bytes 3342336 | tf_op jit(solution)/shard_map/reduce_scatter | solution.py:101
  334.3 1.9 copy-start.2
  392.6 92.0 %copy-start.1 = (bf16[1,36,128,128]{3,2,1,0:T(8,128)(2,1)S(1)}, bf16[1,36,128,128]{3,2,1,0:T(8,128)(2,1)}, u32[]{:S(2)}) copy-start(bf16[1,36,128,128]{3,2,1,0:T(8,128)(2,1)} %param.11) | copy-start | bytes 3538948
Sparse Core Ops, SparseCore 0:
  10.4 54.6 all-gather.8
  67.5 51.0 all-gather.4
  121.0 44.8 reduce-scatter.14
  168.2 45.6 reduce-scatter.12
  216.8 52.1 all-gather.6
  271.0 53.6 all-gather.10
  329.3 76.6 reduce-scatter.8
  410.5 74.0 reduce-scatter.10
where the time goes:
time: 500 us; the launch traced here: 492 us
  waiting for transfers between devices  339 us (68%)
  local copies, waits for them, and re-layouts  70.6 us (14%)
  matrix products  63.4 us (13%)
  between operations  14.7 us (3%)
    all_gather x2, waiting for transfers between devices, row_collect(): return lax.all_gather(field_part, 'row', axis=0, tiled=True)  97.3 us
    unnamed x10, waiting for transfers between devices  83.5 us
    reduce_scatter x2, waiting for transfers between devices, col_sum(): lax.psum_scatter(action(jnp.int32(0), col_share * lax.axis_size('col')).a...  81.7 us
    all_gather x1, waiting for transfers between devices, local(): lax.all_gather(cotangent, 'col', axis=0, tiled=True)  45.8 us
    all_gather x1, waiting for transfers between devices, local(): lax.all_gather(tokens, 'col', axis=0, tiled=True)  31.1 us
    gather x4, local copies, waits for them, and re-layouts, pick_blocks(): return jnp.take(grouped, jnp.maximum(choose, 0), axis=1)  25.8 us
    dot_general x2, matrix products, slot_grads(): jnp.einsum('tcr,tck->crk', left_picked, right_picked, preferred_element_t...  21.5 us
    dot_general x2, matrix products, times_tile(): return jnp.dot(source, tile_matrix, preferred_element_type=jnp.float32)  19.3 us
  transfers between devices with their start and end apart: 8, of which 8 were waited for; matrix products, arithmetic and copies ran while one was open for 27% of the time, Pallas kernels for 0%

commit v1 on v0

v1 whole, which is shorter than its diff:
```python
import functools

import jax
import jax.numpy as jnp
from jax import lax
from jax.experimental import pallas as pl
from jax.experimental.pallas import tpu as pltpu
from jax.sharding import PartitionSpec as P

MESH = pl.DeviceIdType.MESH
BLK = 128
TILE = 12
SIDE = BLK * TILE
CAP = 36
TOKENS = 1024
STAGES = 4
ROWS = TOKENS // STAGES
ROW_SHARE = ROWS // 8
COL_SHARE = ROWS // 16
WIDE = 512
CURVE = 0.7978845608028654
CUBIC = 0.044715
PLAIN = (((1,), (0,)), ((), ()))
FLIPPED = (((1,), (1,)), ((), ()))
TALL = (((0,), (0,)), ((), ()))
COL_GATHER, CORE_GATHER, ROW_SUM, ROW_GATHER, CORE_SUM, COL_SUM, COPIES = 0, 7, 8, 15, 22, 23, 30


def plan():
    order = [("assemble", 0, 0)]
    waiting = []
    chain = (
        "gather_mid", "gather_pass", "gather_core", "rise", "sum_mid", "sum_pair", "sum_end",
        "spread_mid", "spread_pass", "spread_end", "fall", "core_end", "out_mid", "out_pair", "out_end",
    )
    for s in range(STAGES):
        for a in range(2):
            waiting.append((s, a))
    begun = {}
    order.append(("gather", 0, 0))
    order.append(("gather", 0, 1))
    order.append(("assemble", 0, 1))
    for index, (s, a) in enumerate(waiting):
        for depth, name in enumerate(chain):
            begun[(index * 4 + depth, index, depth)] = (name, s, a)
    for key in sorted(begun):
        name, s, a = begun[key]
        if name == "gather_mid" and s + 1 < STAGES:
            order.append((name, s, a))
            order.append(("gather", s + 1, a))
        else:
            order.append((name, s, a))
        if name == "rise":
            order.append(("flip", s, a))
        if name == "spread_end" and s == STAGES - 1:
            order.append(("slots", 0, a))
    return order


def body(
    places, widen_at, narrow_at, tokens, cotangent, widen_blocks, narrow_blocks,
    layer_output, token_grad, widen_grad, narrow_grad,
    gathered, terms, fields, tiles, row_one, row_two, row_pair, row_send, core_in,
    col_one, col_two, col_pair, col_send, hidden, spare, flipped, dense, send_sem, recv_sem,
):
    row, col = lax.axis_index("row"), lax.axis_index("col")
    y_lo, z = row // 4, row % 4
    x, y_hi, core = col // 4, (col // 2) % 2, col % 2

    def on_row(pair, ring):
        return (pair * 4 + ring % 4, col)

    def on_col(ring, pair, side):
        return (row, (ring % 4) * 4 + pair * 2 + side)

    z_next, z_back, y_near = on_row(y_lo, z + 1), on_row(y_lo, z + 3), on_row(1 - y_lo, z)
    x_next, x_back = on_col(x + 1, y_hi, core), on_col(x + 3, y_hi, core)
    y_far, other_core = on_col(x, 1 - y_hi, core), on_col(x, y_hi, 1 - core)

    barrier = pltpu.get_barrier_semaphore()
    partners = (z_next, z_back, y_near, x_next, x_back, y_far, other_core)
    for partner in partners:
        pl.semaphore_signal(barrier, inc=1, device_id=partner, device_id_type=MESH)
    pl.semaphore_wait(barrier, len(partners))

    copies = {}

    def send(s, a, k, source, target, device):
        copy = pltpu.make_async_remote_copy(
            src_ref=source, dst_ref=target, send_sem=send_sem.at[a, s, k], recv_sem=recv_sem.at[a, s, k],
            device_id=device, device_id_type=MESH,
        )
        copy.start()
        copies[s, a, k] = copy

    def arrived(s, a, *ks):
        for k in ks:
            copies[s, a, k].wait_recv()

    def span(ref, a, s, start, length):
        return ref.at[a, s, pl.ds(pl.multiple_of(start, length), length)]

    class Ring:
        def __init__(self, place, pair, share, base, ahead, behind, partner):
            self.place, self.pair, self.share, self.base = place, pair, share, base
            self.ahead, self.behind, self.partner = ahead, behind, partner

        def piece(self, ref, a, s, step, pair):
            return span(ref, a, s, self.base + (((self.place + step) % 4) * 2 + pair) * self.share, self.share)

        def spread(self, ref, s, a, k):
            own = self.piece(ref, a, s, 0, self.pair)
            send(s, a, k, own, own, self.partner)
            send(s, a, k + 1, own, own, self.ahead)
            send(s, a, k + 2, own, own, self.behind)

        def spread_mid(self, ref, s, a, k):
            arrived(s, a, k)
            near = self.piece(ref, a, s, 0, 1 - self.pair)
            send(s, a, k + 3, near, near, self.ahead)
            send(s, a, k + 4, near, near, self.behind)

        def spread_pass(self, ref, s, a, k):
            arrived(s, a, k + 1)
            left = self.piece(ref, a, s, 3, self.pair)
            send(s, a, k + 5, left, left, self.ahead)
            arrived(s, a, k + 4)
            right = self.piece(ref, a, s, 1, 1 - self.pair)
            send(s, a, k + 6, right, right, self.behind)

        def spread_end(self, s, a, k):
            arrived(s, a, k + 2, k + 3, k + 5, k + 6)

        def total(self, ref, one, two, s, a, k):
            size = self.share
            send(s, a, k, self.piece(ref, a, s, 2, 0), span(one, a, s, 0, size), self.ahead)
            send(s, a, k + 1, self.piece(ref, a, s, 2, 1), span(one, a, s, size, size), self.behind)
            send(s, a, k + 2, self.piece(ref, a, s, 1, 1), span(two, a, s, size, size), self.ahead)
            send(s, a, k + 3, self.piece(ref, a, s, 3, 0), span(two, a, s, 2 * size, size), self.behind)

        def total_mid(self, ref, one, two, s, a, k):
            size = self.share
            arrived(s, a, k)
            there = self.piece(ref, a, s, 1, 0)
            add_into(there, [there, span(one, a, s, 0, size)], size)
            send(s, a, k + 4, there, span(two, a, s, 0, size), self.ahead)
            arrived(s, a, k + 1)
            there = self.piece(ref, a, s, 3, 1)
            add_into(there, [there, span(one, a, s, size, size)], size)
            send(s, a, k + 5, there, span(two, a, s, 3 * size, size), self.behind)

        def addends(self, ref, two, s, a, pair):
            size = self.share
            return [
                self.piece(ref, a, s, 0, pair), span(two, a, s, pair * size, size),
                span(two, a, s, (2 + pair) * size, size),
            ]

        def total_pair(self, ref, two, outgoing, incoming, s, a, k):
            arrived(s, a, k + 2, k + 3, k + 4, k + 5)
            add_into(outgoing.at[a, s], self.addends(ref, two, s, a, 1 - self.pair), self.share)
            send(s, a, k + 6, outgoing.at[a, s], incoming.at[a, s], self.partner)

        def total_end(self, ref, two, incoming, s, a, k):
            arrived(s, a, k + 6)
            return self.addends(ref, two, s, a, self.pair) + [incoming.at[a, s]]

    def add_into(target, refs, count):
        @pl.loop(0, count // 16)
        def _(i):
            part = pl.ds(pl.multiple_of(i * 16, 16), 16)
            value = refs[0][part].astype(jnp.float32)
            for ref in refs[1:]:
                value = value + ref[part].astype(jnp.float32)
            target[part] = value.astype(target.dtype)

    row_ring = Ring(z, y_lo, ROW_SHARE, 0, z_next, z_back, y_near)
    col_ring = Ring(x, y_hi, COL_SHARE, core * (ROWS // 2), x_next, x_back, y_far)
    inputs, outputs = (tokens, cotangent), (layer_output, token_grad)

    def product(source, tile, dims, target):
        @pl.loop(0, SIDE // WIDE)
        def _(j):
            part = pl.ds(pl.multiple_of(j * WIDE, WIDE), WIDE)
            other = tiles[tile, :, part] if dims is PLAIN else tiles[tile, part, :]
            target[:, part] = lax.dot_general(
                source[...], other, dims, preferred_element_type=jnp.float32
            ).astype(jnp.bfloat16)

    def assemble(s, a):
        blocks = (widen_blocks, narrow_blocks)[a]
        spare[CAP] = jnp.zeros((BLK, BLK), jnp.bfloat16)

        @pl.loop(0, CAP)
        def _(i):
            spare[i] = blocks[0, i]

        @pl.loop(0, TILE)
        def _(i):
            for j in range(TILE):
                tiles[a, pl.ds(pl.multiple_of(i * BLK, BLK), BLK), j * BLK:(j + 1) * BLK] = spare[
                    places[a, i * TILE + j]
                ]

    def gather(s, a):
        own = col_ring.piece(gathered, a, s, 0, y_hi)
        own[...] = inputs[a][s * COL_SHARE:(s + 1) * COL_SHARE]
        col_ring.spread(gathered, s, a, COL_GATHER)

    def gather_mid(s, a):
        col_ring.spread_mid(gathered, s, a, COL_GATHER)

    def gather_pass(s, a):
        col_ring.spread_pass(gathered, s, a, COL_GATHER)

    def gather_core(s, a):
        col_ring.spread_end(s, a, COL_GATHER)
        half = span(gathered, a, s, core * (ROWS // 2), ROWS // 2)
        send(s, a, CORE_GATHER, half, half, other_core)

    def rise(s, a):
        arrived(s, a, CORE_GATHER)
        product(gathered.at[a, s], a, (PLAIN, FLIPPED)[a], terms.at[a, s])
        row_ring.total(terms, row_one, row_two, s, a, ROW_SUM)

    def sum_mid(s, a):
        row_ring.total_mid(terms, row_one, row_two, s, a, ROW_SUM)

    def sum_pair(s, a):
        row_ring.total_pair(terms, row_two, row_send, row_pair, s, a, ROW_SUM)

    def sum_end(s, a):
        refs = row_ring.total_end(terms, row_two, row_pair, s, a, ROW_SUM)
        own = row_ring.piece(fields, a, s, 0, y_lo)

        @pl.loop(0, ROW_SHARE // 16)
        def _(i):
            part = pl.ds(pl.multiple_of(i * 16, 16), 16)
            value = refs[0][part].astype(jnp.float32)
            for ref in refs[1:]:
                value = value + ref[part].astype(jnp.float32)
            if a == 0:
                hidden[s, part] = value
                bend = jnp.tanh(CURVE * (value + CUBIC * (value * value * value)))
                own[part] = (0.5 * value * (1.0 + bend)).astype(jnp.bfloat16)
            else:
                at = hidden[s, part]
                square = at * at
                bend = jnp.tanh(CURVE * (at + CUBIC * (square * at)))
                slope = 0.5 * (1.0 + bend) + 0.5 * at * (1.0 - bend * bend) * CURVE * (1.0 + 3.0 * CUBIC * square)
                own[part] = (slope * value).astype(jnp.bfloat16)

        row_ring.spread(fields, s, a, ROW_GATHER)

    def spread_mid(s, a):
        row_ring.spread_mid(fields, s, a, ROW_GATHER)

    def spread_pass(s, a):
        row_ring.spread_pass(fields, s, a, ROW_GATHER)

    def spread_end(s, a):
        row_ring.spread_end(s, a, ROW_GATHER)

    def fall(s, a):
        for k in range(ROW_SUM, ROW_SUM + 6):
            copies.pop((s, a, k)).wait_send()
        product(fields.at[a, s], 1 - a, (PLAIN, FLIPPED)[a], terms.at[a, s])
        half = span(terms, a, s, (1 - core) * (ROWS // 2), ROWS // 2)
        send(s, a, CORE_SUM, half, core_in.at[a, s], other_core)

    def core_end(s, a):
        arrived(s, a, CORE_SUM)
        half = span(terms, a, s, core * (ROWS // 2), ROWS // 2)
        add_into(half, [half, core_in.at[a, s]], ROWS // 2)
        col_ring.total(terms, col_one, col_two, s, a, COL_SUM)

    def out_mid(s, a):
        col_ring.total_mid(terms, col_one, col_two, s, a, COL_SUM)

    def out_pair(s, a):
        col_ring.total_pair(terms, col_two, col_send, col_pair, s, a, COL_SUM)

    def out_end(s, a):
        refs = col_ring.total_end(terms, col_two, col_pair, s, a, COL_SUM)
        add_into(outputs[a].at[pl.ds(s * COL_SHARE, COL_SHARE)], refs, COL_SHARE)

    def flip(s, a):
        source = gathered.at[a, s]

        @pl.loop(0, TILE)
        def _(i):
            part = pl.ds(pl.multiple_of(i * BLK, BLK), BLK)
            flipped[a, part, s * ROWS:(s + 1) * ROWS] = source[:, part].T

    def slots(s, a):
        at, target = (narrow_at, widen_at)[a], (narrow_grad, widen_grad)[a]
        dense[TILE * TILE] = jnp.zeros((BLK, BLK), jnp.bfloat16)

        @pl.loop(0, SIDE // WIDE)
        def _(j):
            part = pl.ds(pl.multiple_of(j * WIDE, WIDE), WIDE)
            right = fields[a, :, :, part].reshape(TOKENS, WIDE)

            @pl.loop(0, SIDE // WIDE)
            def _(i):
                value = lax.dot_general(
                    flipped[1 - a, pl.ds(pl.multiple_of(i * WIDE, WIDE), WIDE), :], right, PLAIN,
                    preferred_element_type=jnp.float32,
                )
                value = (value * (1.0 / 32.0)).astype(jnp.bfloat16)
                for r in range(WIDE // BLK):
                    for c in range(WIDE // BLK):
                        place = (i * (WIDE // BLK) + r) * TILE + j * (WIDE // BLK) + c
                        dense[place] = value[r * BLK:(r + 1) * BLK, c * BLK:(c + 1) * BLK]

        @pl.loop(0, CAP // 4)
        def _(g):
            for u in range(4):
                block = dense[at[g * 4 + u]]
                target[0, g * 4 + u] = block.T if a == 0 else block

    steps = {
        step.__name__: step
        for step in (
            assemble, gather, gather_mid, gather_pass, gather_core, rise, sum_mid, sum_pair, sum_end, spread_mid,
            spread_pass, spread_end, fall, core_end, out_mid, out_pair, out_end, flip, slots,
        )
    }
    for name, s, a in plan():
        steps[name](s, a)
    for copy in copies.values():
        copy.wait_send()


def local(tokens, widen_blocks, widen_pattern, narrow_blocks, narrow_pattern, cotangent):
    pattern = jnp.stack([widen_pattern[0], narrow_pattern[0]])
    flat = jnp.where(pattern[..., 0] >= 0, pattern[..., 0] * TILE + pattern[..., 1], -1)
    match = flat[:, :, None] == jnp.arange(TILE * TILE, dtype=jnp.int32)
    slot = jnp.arange(CAP, dtype=jnp.int32)[None, :, None]
    places = jnp.min(jnp.where(match, slot, CAP), axis=1)
    blocks = jnp.where(pattern[..., 0] >= 0, jnp.stack([flat[0], pattern[1, :, 1] * TILE + pattern[1, :, 0]]), TILE * TILE)
    vmem, smem = pl.BlockSpec(memory_space=pltpu.VMEM), pl.BlockSpec(memory_space=pltpu.SMEM)

    def room(*shape, dtype=jnp.bfloat16):
        return pltpu.VMEM((*shape, SIDE), dtype)

    outs = pl.pallas_call(
        body,
        out_shape=(
            jax.ShapeDtypeStruct(tokens.shape, jnp.bfloat16),
            jax.ShapeDtypeStruct(tokens.shape, jnp.bfloat16),
            jax.ShapeDtypeStruct(widen_blocks.shape, jnp.bfloat16),
            jax.ShapeDtypeStruct(narrow_blocks.shape, jnp.bfloat16),
        ),
        in_specs=[smem] * 3 + [vmem] * 4,
        out_specs=[vmem] * 4,
        scratch_shapes=[
            room(2, STAGES, ROWS),
            room(2, STAGES, ROWS),
            room(2, STAGES, ROWS),
            room(2, SIDE),
            room(2, STAGES, 2 * ROW_SHARE),
            room(2, STAGES, 4 * ROW_SHARE),
            room(2, STAGES, ROW_SHARE),
            room(2, STAGES, ROW_SHARE),
            room(2, STAGES, ROWS // 2),
            room(2, STAGES, 2 * COL_SHARE),
            room(2, STAGES, 4 * COL_SHARE),
            room(2, STAGES, COL_SHARE),
            room(2, STAGES, COL_SHARE),
            room(STAGES, ROW_SHARE, dtype=jnp.float32),
            pltpu.VMEM((CAP + 1, BLK, BLK), jnp.bfloat16),
            pltpu.VMEM((2, SIDE, TOKENS), jnp.bfloat16),
            pltpu.VMEM((TILE * TILE + 1, BLK, BLK), jnp.bfloat16),
            pltpu.SemaphoreType.DMA((2, STAGES, COPIES)),
            pltpu.SemaphoreType.DMA((2, STAGES, COPIES)),
        ],
        compiler_params=pltpu.CompilerParams(
            collective_id=0, has_side_effects=True, vmem_limit_bytes=62 * 2**20
        ),
        name="layer",
    )(
        places, blocks[0], blocks[1], tokens, cotangent, widen_blocks, narrow_blocks,
    )
    return outs


def solution(mesh):
    placed = (
        P("col", "row"),
        P("row", "col", None, None),
        P("row", "col", None),
        P("row", "col", None, None),
        P("row", "col", None),
        P("col", "row"),
    )
    return jax.shard_map(
        local,
        mesh=mesh,
        in_specs=placed,
        out_specs=(
            P("col", "row"),
            P("col", "row"),
            P("row", "col", None, None),
            P("row", "col", None, None),
        ),
        check_vma=False,
    )
```

time: 500 us -> 228 us (0.46); the launches traced: 492 us -> 227 us
  waiting for transfers between devices: 339 us -> 0 us
  Pallas kernels: 0 us -> 216 us
  matrix products: 63.4 us -> 0 us
  local copies, waits for them, and re-layouts: 70.6 us -> 8.74 us
  between operations: 14.7 us -> 0.66 us
    pallas_call x0 -> x1, Pallas kernels: none -> 216 us  [local(): pl.pallas_call(body, out_shape=(jax.ShapeDtypeStruct(tokens.shape, jnp.bf...]
    all_gather x4 -> x0, waiting for transfers between devices: 174 us -> none  [the longest x2 97.3 us: row_collect(): return lax.all_gather(field_part, 'row', axis=0, tiled=True)]
    unnamed x10 -> x0, waiting for transfers between devices: 83.5 us -> none
    reduce_scatter x2 -> x0, waiting for transfers between devices: 81.7 us -> none  [col_sum(): lax.psum_scatter(action(jnp.int32(0), col_share * lax.axis_size('col')).a...]
    dot_general x8 -> x0, matrix products: 63.4 us -> none  [the longest x2 21.5 us: slot_grads(): jnp.einsum('tcr,tck->crk', left_picked, right_picked, preferred_element_t...]
    gather x4 -> x0, local copies, waits for them, and re-layouts: 25.8 us -> none  [pick_blocks(): return jnp.take(grouped, jnp.maximum(choose, 0), axis=1)]
    transpose x2 -> x0, local copies, waits for them, and re-layouts: 12.7 us -> none  [dense_tile(): placed.transpose(0, 2, 1, 3).reshape(in_count * side, out_count * side)]
    reshape x3 -> x0, local copies, waits for them, and re-layouts: 11.8 us -> none  [pick_blocks(): grouped = source.reshape(height, number, source.shape[1] // number)]
  transfers between devices with their start and end apart: 8 -> 0, of which waited for: 8 -> 0; matrix products, arithmetic and copies ran while one was open for 27% -> 0% of each run, Pallas kernels for 0% -> 0%
where the time goes in v1:
time: 228 us; the launch traced here: 227 us
  Pallas kernels  216 us (95%)
  local copies, waits for them, and re-layouts  8.74 us (4%)
    pallas_call x1, Pallas kernels, local(): pl.pallas_call(body, out_shape=(jax.ShapeDtypeStruct(tokens.shape, jnp.bf...  216 us
    unnamed x7, local copies, waits for them, and re-layouts  7.43 us

profile of v1, /device:TPU:0, one launch (start us, length us, event | category | flops | bytes accessed | tf_op | source)
XLA Modules:
  0.0 226.8 jit_solution(3944292738139271258)
XLA Ops:
  0.6 0.8 add_bitcast_fusion
  1.4 0.7 constant_dynamic-update-slice_fusion.1
  2.1 0.7 constant_dynamic-update-slice_fusion
  2.8 0.5 slice_bitcast_fusion
  3.3 0.1 copy.10
  3.4 0.7 fusion.places
  4.1 215.9 %layer.1 = (bf16[64,1536]{1,0:T(8,128)(2,1)}, bf16[64,1536]{1,0:T(8,128)(2,1)}, bf16[1,36,128,128]{3,2,1,0:T(8,128)(2,1)}, bf16[1,36,128,128]{3,2,1,0:T(8,128)(2,1)}) custom-call(s32[2,144]{1,0:T(2,128)} %fusion.places, s32[36]{0:T(128)} %get-tuple-element.7.widen_at, s32[36]{0:T(128)} %get-tuple-element.6.narrow_at, bf16[64,1536]{1,0:T(8,128)(2,1)} %tokens.1, ...), custom_call_target="tpu_custom_call" | custom-call | tf_op jit(solution)/shard_map/layer/pallas_call | solution.py:347
  220.0 1.6 copy.19
  221.6 1.6 copy.20
  223.3 0.0 copy-start
  223.3 2.5 %copy.21 = bf16[1,36,128,128]{3,2,1,0:T(8,128)(2,1)} copy(bf16[1,36,128,128]{3,2,1,0:T(8,128)(2,1)} %get-tuple-element.14) | data formatting | bytes 2359296
  225.8 0.0 copy-done
  225.8 1.0 copy.22
  (5 shorter events, 0.0 us)
Async XLA Ops:
  223.3 2.5 %copy-start = (bf16[1,36,128,128]{3,2,1,0:T(8,128)(2,1)S(1)}, bf16[1,36,128,128]{3,2,1,0:T(8,128)(2,1)}, u32[]{:S(2)}) copy-start(bf16[1,36,128,128]{3,2,1,0:T(8,128)(2,1)} %get-tuple-element.15) | copy-start | bytes 3538948

commit v2 on v1

--- a/solution.py
+++ b/solution.py
@@ -23,38 +23,34 @@
 PLAIN = (((1,), (0,)), ((), ()))
 FLIPPED = (((1,), (1,)), ((), ()))
 TALL = (((0,), (0,)), ((), ()))
-COL_GATHER, CORE_GATHER, ROW_SUM, ROW_GATHER, CORE_SUM, COL_SUM, COPIES = 0, 7, 8, 15, 22, 23, 30
-
-
-def plan():
-    order = [("assemble", 0, 0)]
-    waiting = []
-    chain = (
-        "gather_mid", "gather_pass", "gather_core", "rise", "sum_mid", "sum_pair", "sum_end",
-        "spread_mid", "spread_pass", "spread_end", "fall", "core_end", "out_mid", "out_pair", "out_end",
-    )
-    for s in range(STAGES):
-        for a in range(2):
-            waiting.append((s, a))
-    begun = {}
-    order.append(("gather", 0, 0))
-    order.append(("gather", 0, 1))
-    order.append(("assemble", 0, 1))
-    for index, (s, a) in enumerate(waiting):
-        for depth, name in enumerate(chain):
-            begun[(index * 4 + depth, index, depth)] = (name, s, a)
-    for key in sorted(begun):
-        name, s, a = begun[key]
-        if name == "gather_mid" and s + 1 < STAGES:
-            order.append((name, s, a))
-            order.append(("gather", s + 1, a))
-        else:
-            order.append((name, s, a))
-        if name == "rise":
-            order.append(("flip", s, a))
-        if name == "spread_end" and s == STAGES - 1:
-            order.append(("slots", 0, a))
-    return order
+COL_GATHER, CORE_GATHER, ROW_SUM, ROW_GATHER, CORE_SUM, COL_SUM, COPIES = 0, 7, 8, 18, 26, 27, 34
+
+
+NEAR = ((0, 0), (0, 1), (2, 0))
+WIDE_FIRST = ((0, 0), (0, 1), (1, 0))
+STEPS = (
+    "gather", "assemble", "gather_mid", "gather_pass", "gather_core", "rise", "sumb_two", "sum_mid", "sumb_one",
+    "sumb_mid", "sum_pair", "sumb_end", "sum_end", "sprb_mid", "flip", "sprb_pass", "spread_mid", "sprb_end", "fall",
+    "spread_pass", "core_end", "out_mid", "spread_end", "out_pair", "slot", "out_end", "pick",
+)
+ORDER = (
+    (0, 0, 0), (0, 1, 0), (1, 0, 0), (0, 2, 0), (2, 0, 0), (2, 1, 0), (2, 2, 0), (0, 3, 0), (3, 0, 0), (3, 1, 0),
+    (2, 3, 0), (3, 2, 0), (0, 0, 1), (1, 0, 1), (4, 0, 0), (0, 1, 1), (4, 1, 0), (3, 3, 0), (5, 0, 0), (4, 2, 0),
+    (5, 1, 0), (4, 3, 0), (0, 2, 1), (0, 3, 1), (5, 2, 0), (6, 0, 0), (2, 1, 1), (7, 1, 0), (2, 0, 1), (5, 3, 0),
+    (3, 0, 1), (8, 0, 0), (3, 1, 1), (9, 0, 0), (10, 1, 0), (2, 2, 1), (4, 0, 1), (7, 3, 0), (3, 2, 1), (6, 2, 0),
+    (2, 3, 1), (5, 0, 1), (4, 2, 1), (8, 2, 0), (11, 0, 0), (10, 3, 0), (9, 2, 0), (5, 2, 1), (12, 1, 0), (13, 0, 0),
+    (3, 3, 1), (11, 2, 0), (14, 0, 1), (6, 0, 1), (4, 3, 1), (7, 2, 1), (4, 1, 1), (14, 3, 0), (8, 0, 1), (5, 3, 1),
+    (13, 1, 0), (5, 1, 1), (14, 1, 1), (12, 3, 0), (9, 0, 1), (14, 1, 0), (10, 2, 1), (14, 3, 1), (14, 0, 0),
+    (14, 2, 0), (14, 2, 1), (7, 3, 1), (15, 0, 0), (16, 2, 0), (15, 1, 0), (7, 1, 1), (16, 3, 0), (11, 0, 1),
+    (12, 2, 1), (10, 3, 1), (17, 0, 0), (18, 0, 0), (19, 2, 0), (17, 1, 0), (18, 1, 0), (10, 1, 1), (20, 0, 0),
+    (19, 3, 0), (16, 2, 1), (20, 1, 0), (21, 0, 0), (12, 3, 1), (13, 0, 1), (21, 1, 0), (12, 1, 1), (22, 2, 0),
+    (18, 2, 0), (23, 0, 0), (22, 3, 0), (18, 3, 0), (19, 2, 1), (20, 2, 0), (16, 3, 1), (24, 0, 0), (20, 3, 0),
+    (15, 0, 1), (21, 2, 0), (16, 1, 1), (25, 0, 0), (23, 1, 0), (24, 1, 0), (22, 2, 1), (18, 2, 1), (23, 2, 0),
+    (17, 0, 1), (18, 0, 1), (19, 1, 1), (19, 3, 1), (20, 2, 1), (21, 3, 0), (24, 2, 0), (20, 0, 1), (21, 2, 1),
+    (22, 1, 1), (18, 1, 1), (22, 3, 1), (18, 3, 1), (21, 0, 1), (23, 3, 0), (20, 1, 1), (23, 2, 1), (26, 0, 0),
+    (20, 3, 1), (24, 0, 1), (25, 3, 0), (21, 1, 1), (21, 3, 1), (25, 1, 0), (23, 0, 1), (24, 1, 1), (23, 1, 1),
+    (23, 3, 1), (24, 2, 1), (25, 0, 1), (25, 2, 0), (25, 2, 1), (25, 1, 1), (26, 0, 1), (25, 3, 1),
+)
 
 
 def body(
@@ -130,6 +126,77 @@
 
         def spread_end(self, s, a, k):
             arrived(s, a, k + 2, k + 3, k + 5, k + 6)
+
+        def half(self, ref, which):
+            size = self.share // 2
+            return ref.at[pl.ds(which * size, size)]
+
+        def wide(self, ref, s, a, k):
+            own = self.piece(ref, a, s, 0, self.pair)
+            send(s, a, k, own, own, self.ahead)
+            send(s, a, k + 1, own, own, self.behind)
+            send(s, a, k + 4, own, own, self.partner)
+
+        def wide_mid(self, ref, s, a, k):
+            left, right = self.piece(ref, a, s, 3, self.pair), self.piece(ref, a, s, 1, self.pair)
+            arrived(s, a, k)
+            send(s, a, k + 2, self.half(left, 0), self.half(left, 0), self.ahead)
+            arrived(s, a, k + 1)
+            send(s, a, k + 3, self.half(right, 1), self.half(right, 1), self.behind)
+            send(s, a, k + 5, left, left, self.partner)
+            send(s, a, k + 6, right, right, self.partner)
+
+        def wide_pass(self, ref, s, a, k):
+            arrived(s, a, k + 2, k + 3)
+            far = self.piece(ref, a, s, 2, self.pair)
+            send(s, a, k + 7, far, far, self.partner)
+
+        def wide_end(self, s, a, k):
+            arrived(s, a, k + 4, k + 5, k + 6, k + 7)
+
+        def near(self, ref, near, s, a, k):
+            for i, step in enumerate((2, 1, 3, 0)):
+                source = self.piece(ref, a, s, step, 1 - self.pair)
+                send(s, a, k + i, source, span(near, a, s, step * self.share, self.share), self.partner)
+
+        def join(self, ref, near, s, a, step):
+            there = self.piece(ref, a, s, step, self.pair)
+            add_into(there, [there, span(near, a, s, step * self.share, self.share)], self.share)
+            return there
+
+        def near_two(self, ref, near, one, s, a, k):
+            arrived(s, a, k)
+            there = self.join(ref, near, s, a, 2)
+            send(s, a, k + 4, self.half(there, 0), self.half(one.at[a, s], 0), self.ahead)
+            send(s, a, k + 5, self.half(there, 1), self.half(one.at[a, s], 1), self.behind)
+
+        def near_one(self, ref, near, two, s, a, k):
+            size = self.share
+            arrived(s, a, k + 1)
+            there = self.join(ref, near, s, a, 1)
+            send(s, a, k + 6, self.half(there, 1), self.half(span(two, a, s, 0, size), 1), self.ahead)
+            arrived(s, a, k + 2)
+            there = self.join(ref, near, s, a, 3)
+            send(s, a, k + 7, self.half(there, 0), self.half(span(two, a, s, size, size), 0), self.behind)
+
+        def near_mid(self, ref, one, two, s, a, k):
+            size = self.share
+            arrived(s, a, k + 4)
+            there = self.half(self.piece(ref, a, s, 1, self.pair), 0)
+            add_into(there, [there, self.half(one.at[a, s], 0)], size // 2)
+            send(s, a, k + 8, there, self.half(span(two, a, s, 0, size), 0), self.ahead)
+            arrived(s, a, k + 5)
+            there = self.half(self.piece(ref, a, s, 3, self.pair), 1)
+            add_into(there, [there, self.half(one.at[a, s], 1)], size // 2)
+            send(s, a, k + 9, there, self.half(span(two, a, s, size, size), 1), self.behind)
+
+        def near_end(self, ref, near, two, s, a, k):
+            size = self.share
+            arrived(s, a, k + 3, k + 6, k + 7, k + 8, k + 9)
+            return [
+                self.piece(ref, a, s, 0, self.pair), span(near, a, s, 0, size),
+                span(two, a, s, 0, size), span(two, a, s, size, size),
+            ]
 
         def total(self, ref, one, two, s, a, k):
             size = self.share
@@ -221,7 +288,10 @@
     def rise(s, a):
         arrived(s, a, CORE_GATHER)
         product(gathered.at[a, s], a, (PLAIN, FLIPPED)[a], terms.at[a, s])
-        row_ring.total(terms, row_one, row_two, s, a, ROW_SUM)
+        if (s, a) in NEAR:
+            row_ring.near(terms, row_two, s, a, ROW_SUM)
+        else:
+            row_ring.total(terms, row_one, row_two, s, a, ROW_SUM)
 
     def sum_mid(s, a):
         row_ring.total_mid(terms, row_one, row_two, s, a, ROW_SUM)
@@ -229,8 +299,22 @@
     def sum_pair(s, a):
         row_ring.total_pair(terms, row_two, row_send, row_pair, s, a, ROW_SUM)
 
+    def sumb_two(s, a):
+        row_ring.near_two(terms, row_two, row_pair, s, a, ROW_SUM)
+
+    def sumb_one(s, a):
+        row_ring.near_one(terms, row_two, row_one, s, a, ROW_SUM)
+
+    def sumb_mid(s, a):
+        row_ring.near_mid(terms, row_pair, row_one, s, a, ROW_SUM)
+
+    def sumb_end(s, a):
+        bend_fields(s, a, row_ring.near_end(terms, row_two, row_one, s, a, ROW_SUM))
+
     def sum_end(s, a):
-        refs = row_ring.total_end(terms, row_two, row_pair, s, a, ROW_SUM)
+        bend_fields(s, a, row_ring.total_end(terms, row_two, row_pair, s, a, ROW_SUM))
+
+    def bend_fields(s, a, refs):
         own = row_ring.piece(fields, a, s, 0, y_lo)
 
         @pl.loop(0, ROW_SHARE // 16)
@@ -250,7 +334,19 @@
                 slope = 0.5 * (1.0 + bend) + 0.5 * at * (1.0 - bend * bend) * CURVE * (1.0 + 3.0 * CUBIC * square)
                 own[part] = (slope * value).astype(jnp.bfloat16)
 
-        row_ring.spread(fields, s, a, ROW_GATHER)
+        if (s, a) in WIDE_FIRST:
+            row_ring.wide(fields, s, a, ROW_GATHER)
+        else:
+            row_ring.spread(fields, s, a, ROW_GATHER)
+
+    def sprb_mid(s, a):
+        row_ring.wide_mid(fields, s, a, ROW_GATHER)
+
+    def sprb_pass(s, a):
+        row_ring.wide_pass(fields, s, a, ROW_GATHER)
+
+    def sprb_end(s, a):
+        row_ring.wide_end(s, a, ROW_GATHER)
 
     def spread_mid(s, a):
         row_ring.spread_mid(fields, s, a, ROW_GATHER)
@@ -262,8 +358,9 @@
         row_ring.spread_end(s, a, ROW_GATHER)
 
     def fall(s, a):
-        for k in range(ROW_SUM, ROW_SUM + 6):
-            copies.pop((s, a, k)).wait_send()
+        for k in range(ROW_SUM, ROW_GATHER):
+            if (s, a, k) in copies:
+                copies.pop((s, a, k)).wait_send()
         product(fields.at[a, s], 1 - a, (PLAIN, FLIPPED)[a], terms.at[a, s])
         half = span(terms, a, s, (1 - core) * (ROWS // 2), ROWS // 2)
         send(s, a, CORE_SUM, half, core_in.at[a, s], other_core)
@@ -292,26 +389,25 @@
             part = pl.ds(pl.multiple_of(i * BLK, BLK), BLK)
             flipped[a, part, s * ROWS:(s + 1) * ROWS] = source[:, part].T
 
-    def slots(s, a):
+    def slot(j, a):
+        part = pl.ds(j * WIDE, WIDE)
+        right = fields[a, :, :, part].reshape(TOKENS, WIDE)
+
+        @pl.loop(0, SIDE // WIDE)
+        def _(i):
+            value = lax.dot_general(
+                flipped[1 - a, pl.ds(pl.multiple_of(i * WIDE, WIDE), WIDE), :], right, PLAIN,
+                preferred_element_type=jnp.float32,
+            )
+            value = (value * (1.0 / 32.0)).astype(jnp.bfloat16)
+            for r in range(WIDE // BLK):
+                for c in range(WIDE // BLK):
+                    place = (i * (WIDE // BLK) + r) * TILE + j * (WIDE // BLK) + c
+                    dense[place] = value[r * BLK:(r + 1) * BLK, c * BLK:(c + 1) * BLK]
+
+    def pick(s, a):
         at, target = (narrow_at, widen_at)[a], (narrow_grad, widen_grad)[a]
         dense[TILE * TILE] = jnp.zeros((BLK, BLK), jnp.bfloat16)
-
-        @pl.loop(0, SIDE // WIDE)
-        def _(j):
-            part = pl.ds(pl.multiple_of(j * WIDE, WIDE), WIDE)
-            right = fields[a, :, :, part].reshape(TOKENS, WIDE)
-
-            @pl.loop(0, SIDE // WIDE)
-            def _(i):
-                value = lax.dot_general(
-                    flipped[1 - a, pl.ds(pl.multiple_of(i * WIDE, WIDE), WIDE), :], right, PLAIN,
-                    preferred_element_type=jnp.float32,
-                )
-                value = (value * (1.0 / 32.0)).astype(jnp.bfloat16)
-                for r in range(WIDE // BLK):
-                    for c in range(WIDE // BLK):
-                        place = (i * (WIDE // BLK) + r) * TILE + j * (WIDE // BLK) + c
-                        dense[place] = value[r * BLK:(r + 1) * BLK, c * BLK:(c + 1) * BLK]
 
         @pl.loop(0, CAP // 4)
         def _(g):
@@ -323,11 +419,12 @@
         step.__name__: step
         for step in (
             assemble, gather, gather_mid, gather_pass, gather_core, rise, sum_mid, sum_pair, sum_end, spread_mid,
-            spread_pass, spread_end, fall, core_end, out_mid, out_pair, out_end, flip, slots,
+            spread_pass, spread_end, fall, core_end, out_mid, out_pair, out_end, flip, slot, pick,
+            sumb_two, sumb_one, sumb_mid, sumb_end, sprb_mid, sprb_pass, sprb_end,
         )
     }
-    for name, s, a in plan():
-        steps[name](s, a)
+    for index, s, a in ORDER:
+        steps[STEPS[index]](s, a)
     for copy in copies.values():
         copy.wait_send()
 

time: 228 us -> 147 us (0.64)
  Pallas kernels: 216 us -> 136 us
    pallas_call x1, Pallas kernels: 216 us -> 136 us  [local(): pl.pallas_call(body, out_shape=(jax.ShapeDtypeStruct(tokens.shape, jnp.bf...]
where the time goes in v2:
time: 147 us; the launch traced here: 146 us
  Pallas kernels  136 us (93%)
  local copies, waits for them, and re-layouts  8.74 us (6%)
  other arithmetic  1.5 us (1%)
    pallas_call x1, Pallas kernels, local(): pl.pallas_call(body, out_shape=(jax.ShapeDtypeStruct(tokens.shape, jnp.bf...  136 us
    unnamed x7, local copies, waits for them, and re-layouts  7.43 us

profile of v2, /device:TPU:0, one launch (start us, length us, event | category | flops | bytes accessed | tf_op | source)
XLA Modules:
  0.0 146.4 jit_solution(14462468863301605990)
XLA Ops:
  0.6 0.8 add_bitcast_fusion
  1.4 0.7 constant_dynamic-update-slice_fusion.1
  2.1 0.7 constant_dynamic-update-slice_fusion
  2.8 0.5 slice_bitcast_fusion
  3.3 0.1 copy.10
  3.4 0.7 fusion.places
  4.1 135.5 %layer.1 = (bf16[64,1536]{1,0:T(8,128)(2,1)}, bf16[64,1536]{1,0:T(8,128)(2,1)}, bf16[1,36,128,128]{3,2,1,0:T(8,128)(2,1)}, bf16[1,36,128,128]{3,2,1,0:T(8,128)(2,1)}) custom-call(s32[2,144]{1,0:T(2,128)} %fusion.places, s32[36]{0:T(128)} %get-tuple-element.7.widen_at, s32[36]{0:T(128)} %get-tuple-element.6.narrow_at, bf16[64,1536]{1,0:T(8,128)(2,1)} %tokens.1, ...), custom_call_target="tpu_custom_call" | custom-call | tf_op jit(solution)/shard_map/layer/pallas_call | solution.py:444
  139.7 1.6 %copy.19 = bf16[64,1536]{1,0:T(8,128)(2,1)} copy(bf16[64,1536]{1,0:T(8,128)(2,1)} %get-tuple-element.12) | data formatting | bytes 393216
  141.3 1.6 %copy.20 = bf16[64,1536]{1,0:T(8,128)(2,1)} copy(bf16[64,1536]{1,0:T(8,128)(2,1)} %get-tuple-element.13) | data formatting | bytes 393216
  142.9 0.0 copy-start
  142.9 2.5 %copy.21 = bf16[1,36,128,128]{3,2,1,0:T(8,128)(2,1)} copy(bf16[1,36,128,128]{3,2,1,0:T(8,128)(2,1)} %get-tuple-element.14) | data formatting | bytes 2359296
  145.4 0.0 copy-done
  145.4 1.0 copy.22
  (5 shorter events, 0.0 us)
Async XLA Ops:
  142.9 2.5 %copy-start = (bf16[1,36,128,128]{3,2,1,0:T(8,128)(2,1)S(1)}, bf16[1,36,128,128]{3,2,1,0:T(8,128)(2,1)}, u32[]{:S(2)}) copy-start(bf16[1,36,128,128]{3,2,1,0:T(8,128)(2,1)} %get-tuple-element.15) | copy-start | bytes 3538948

commit v3 on v2

--- a/solution.py
+++ b/solution.py
@@ -54,10 +54,11 @@
 
 
 def body(
-    places, widen_at, narrow_at, tokens, cotangent, widen_blocks, narrow_blocks,
+    widen_at, narrow_at, tokens, cotangent, widen_blocks, narrow_blocks,
     layer_output, token_grad, widen_grad, narrow_grad,
     gathered, terms, fields, tiles, row_one, row_two, row_pair, row_send, core_in,
-    col_one, col_two, col_pair, col_send, hidden, spare, flipped, dense, send_sem, recv_sem,
+    col_one, col_two, col_pair, col_send, hidden, widen_spare, narrow_spare, flipped, dense, picked, results, at, marks, places,
+    send_sem, recv_sem, here_sem,
 ):
     row, col = lax.axis_index("row"), lax.axis_index("col")
     y_lo, z = row // 4, row % 4
@@ -73,10 +74,40 @@
     x_next, x_back = on_col(x + 1, y_hi, core), on_col(x + 3, y_hi, core)
     y_far, other_core = on_col(x, 1 - y_hi, core), on_col(x, y_hi, 1 - core)
 
+    spare = (widen_spare, narrow_spare)
+    own_rows = pl.multiple_of(core * (ROWS // 2) + (x * 2 + y_hi) * COL_SHARE, COL_SHARE)
+    loads = {}
+    for i, (source, target) in enumerate((
+        (tokens, gathered.at[0, :, pl.ds(own_rows, COL_SHARE)]),
+        (widen_at, at.at[0]),
+        (narrow_at, at.at[1]),
+        (cotangent, gathered.at[1, :, pl.ds(own_rows, COL_SHARE)]),
+        (widen_blocks.at[0], widen_spare.at[pl.ds(0, CAP)]),
+        (narrow_blocks.at[0], narrow_spare.at[pl.ds(0, CAP)]),
+    )):
+        loads[i] = pltpu.make_async_copy(source, target, here_sem.at[i])
+        loads[i].start()
+
     barrier = pltpu.get_barrier_semaphore()
     partners = (z_next, z_back, y_near, x_next, x_back, y_far, other_core)
     for partner in partners:
         pl.semaphore_signal(barrier, inc=1, device_id=partner, device_id_type=MESH)
+
+    def place(a, i):
+        return (at[a, 0, i] + 1) * TILE + at[a, 1, i] + 1
+
+    count = lax.broadcasted_iota(jnp.int32, (1, 2 * BLK), 1)
+    for a in range(2):
+        loads[1 + a].wait()
+        marks[a:a + 1] = lax.fori_loop(
+            0, CAP, lambda i, mark: jnp.where(count == place(a, i), i, mark), jnp.full((1, 2 * BLK), CAP, jnp.int32)
+        )
+    loads[6] = pltpu.make_async_copy(marks, places, here_sem.at[6])
+    loads[6].start()
+    for a in range(2):
+        spare[a][CAP] = jnp.zeros((BLK, BLK), jnp.bfloat16)
+    dense[0] = jnp.zeros((BLK, BLK), jnp.bfloat16)
+    loads[6].wait()
     pl.semaphore_wait(barrier, len(partners))
 
     copies = {}
@@ -243,7 +274,7 @@
 
     row_ring = Ring(z, y_lo, ROW_SHARE, 0, z_next, z_back, y_near)
     col_ring = Ring(x, y_hi, COL_SHARE, core * (ROWS // 2), x_next, x_back, y_far)
-    inputs, outputs = (tokens, cotangent), (layer_output, token_grad)
+    outputs, stores = (layer_output, token_grad), []
 
     def product(source, tile, dims, target):
         @pl.loop(0, SIDE // WIDE)
@@ -255,23 +286,18 @@
             ).astype(jnp.bfloat16)
 
     def assemble(s, a):
-        blocks = (widen_blocks, narrow_blocks)[a]
-        spare[CAP] = jnp.zeros((BLK, BLK), jnp.bfloat16)
-
-        @pl.loop(0, CAP)
-        def _(i):
-            spare[i] = blocks[0, i]
+        loads[4 + a].wait()
 
         @pl.loop(0, TILE)
         def _(i):
             for j in range(TILE):
-                tiles[a, pl.ds(pl.multiple_of(i * BLK, BLK), BLK), j * BLK:(j + 1) * BLK] = spare[
-                    places[a, i * TILE + j]
+                tiles[a, pl.ds(pl.multiple_of(i * BLK, BLK), BLK), j * BLK:(j + 1) * BLK] = spare[a][
+                    places[a, (i + 1) * TILE + j + 1]
                 ]
 
     def gather(s, a):
-        own = col_ring.piece(gathered, a, s, 0, y_hi)
-        own[...] = inputs[a][s * COL_SHARE:(s + 1) * COL_SHARE]
+        if s == 0:
+            loads[3 * a].wait()
         col_ring.spread(gathered, s, a, COL_GATHER)
 
     def gather_mid(s, a):
@@ -379,7 +405,10 @@
 
     def out_end(s, a):
         refs = col_ring.total_end(terms, col_two, col_pair, s, a, COL_SUM)
-        add_into(outputs[a].at[pl.ds(s * COL_SHARE, COL_SHARE)], refs, COL_SHARE)
+        add_into(results.at[a, s], refs, COL_SHARE)
+        store = pltpu.make_async_copy(results.at[a, s], outputs[a].at[s], here_sem.at[9 + a * STAGES + s])
+        store.start()
+        stores.append(store)
 
     def flip(s, a):
         source = gathered.at[a, s]
@@ -402,18 +431,25 @@
             value = (value * (1.0 / 32.0)).astype(jnp.bfloat16)
             for r in range(WIDE // BLK):
                 for c in range(WIDE // BLK):
-                    place = (i * (WIDE // BLK) + r) * TILE + j * (WIDE // BLK) + c
-                    dense[place] = value[r * BLK:(r + 1) * BLK, c * BLK:(c + 1) * BLK]
+                    spot = (i * (WIDE // BLK) + r + 1) * TILE + j * (WIDE // BLK) + c + 1
+                    dense[spot] = value[r * BLK:(r + 1) * BLK, c * BLK:(c + 1) * BLK]
 
     def pick(s, a):
-        at, target = (narrow_at, widen_at)[a], (narrow_grad, widen_grad)[a]
-        dense[TILE * TILE] = jnp.zeros((BLK, BLK), jnp.bfloat16)
+        target = (narrow_grad, widen_grad)[a]
 
         @pl.loop(0, CAP // 4)
         def _(g):
             for u in range(4):
-                block = dense[at[g * 4 + u]]
-                target[0, g * 4 + u] = block.T if a == 0 else block
+                i = g * 4 + u
+                if a == 0:
+                    row_at, col_at = at[1, 0, i], at[1, 1, i]
+                    picked[a, i] = dense[(col_at + 1) * TILE + row_at + 1].T
+                else:
+                    picked[a, i] = dense[place(0, i)]
+
+        store = pltpu.make_async_copy(picked.at[a], target.at[0], here_sem.at[7 + a])
+        store.start()
+        stores.append(store)
 
     steps = {
         step.__name__: step
@@ -427,30 +463,41 @@
         steps[STEPS[index]](s, a)
     for copy in copies.values():
         copy.wait_send()
+    for store in stores:
+        store.wait()
+
+
+def hand_on(*refs):
+    sources, targets, rooms, sem = refs[:4], refs[4:8], refs[8:12], refs[12]
+    loads = [pltpu.make_async_copy(a, b, sem.at[0, i]) for i, (a, b) in enumerate(zip(sources, rooms))]
+    stores = [pltpu.make_async_copy(a, b, sem.at[1, i]) for i, (a, b) in enumerate(zip(rooms, targets))]
+    for load in loads:
+        load.start()
+    for load, store in zip(loads, stores):
+        load.wait()
+        store.start()
+    for store in stores:
+        store.wait()
 
 
 def local(tokens, widen_blocks, widen_pattern, narrow_blocks, narrow_pattern, cotangent):
-    pattern = jnp.stack([widen_pattern[0], narrow_pattern[0]])
-    flat = jnp.where(pattern[..., 0] >= 0, pattern[..., 0] * TILE + pattern[..., 1], -1)
-    match = flat[:, :, None] == jnp.arange(TILE * TILE, dtype=jnp.int32)
-    slot = jnp.arange(CAP, dtype=jnp.int32)[None, :, None]
-    places = jnp.min(jnp.where(match, slot, CAP), axis=1)
-    blocks = jnp.where(pattern[..., 0] >= 0, jnp.stack([flat[0], pattern[1, :, 1] * TILE + pattern[1, :, 0]]), TILE * TILE)
-    vmem, smem = pl.BlockSpec(memory_space=pltpu.VMEM), pl.BlockSpec(memory_space=pltpu.SMEM)
+    grouped = (STAGES, COL_SHARE, SIDE)
+    anywhere = pl.BlockSpec(memory_space=pl.ANY)
+    results = (
+        jax.ShapeDtypeStruct(grouped, jnp.bfloat16),
+        jax.ShapeDtypeStruct(grouped, jnp.bfloat16),
+        jax.ShapeDtypeStruct(widen_blocks.shape, jnp.bfloat16),
+        jax.ShapeDtypeStruct(narrow_blocks.shape, jnp.bfloat16),
+    )
 
     def room(*shape, dtype=jnp.bfloat16):
         return pltpu.VMEM((*shape, SIDE), dtype)
 
     outs = pl.pallas_call(
         body,
-        out_shape=(
-            jax.ShapeDtypeStruct(tokens.shape, jnp.bfloat16),
-            jax.ShapeDtypeStruct(tokens.shape, jnp.bfloat16),
-            jax.ShapeDtypeStruct(widen_blocks.shape, jnp.bfloat16),
-            jax.ShapeDtypeStruct(narrow_blocks.shape, jnp.bfloat16),
-        ),
-        in_specs=[smem] * 3 + [vmem] * 4,
-        out_specs=[vmem] * 4,
+        out_shape=results,
+        in_specs=[anywhere] * 6,
+        out_specs=[anywhere] * 4,
         scratch_shapes=[
             room(2, STAGES, ROWS),
             room(2, STAGES, ROWS),
@@ -467,19 +514,32 @@
             room(2, STAGES, COL_SHARE),
             room(STAGES, ROW_SHARE, dtype=jnp.float32),
             pltpu.VMEM((CAP + 1, BLK, BLK), jnp.bfloat16),
+            pltpu.VMEM((CAP + 1, BLK, BLK), jnp.bfloat16),
             pltpu.VMEM((2, SIDE, TOKENS), jnp.bfloat16),
-            pltpu.VMEM((TILE * TILE + 1, BLK, BLK), jnp.bfloat16),
+            pltpu.VMEM((TILE * (TILE + 1) + 1, BLK, BLK), jnp.bfloat16),
+            pltpu.VMEM((2, CAP, BLK, BLK), jnp.bfloat16),
+            pltpu.VMEM((2, *grouped), jnp.bfloat16),
+            pltpu.SMEM((2, 2, CAP), jnp.int32),
+            pltpu.VMEM((2, 2 * BLK), jnp.int32),
+            pltpu.SMEM((2, 2 * BLK), jnp.int32),
             pltpu.SemaphoreType.DMA((2, STAGES, COPIES)),
             pltpu.SemaphoreType.DMA((2, STAGES, COPIES)),
+            pltpu.SemaphoreType.DMA((9 + 2 * STAGES,)),
         ],
         compiler_params=pltpu.CompilerParams(
             collective_id=0, has_side_effects=True, vmem_limit_bytes=62 * 2**20
         ),
         name="layer",
     )(
-        places, blocks[0], blocks[1], tokens, cotangent, widen_blocks, narrow_blocks,
+        widen_pattern[0].T, narrow_pattern[0].T, tokens.reshape(grouped), cotangent.reshape(grouped),
+        widen_blocks, narrow_blocks,
     )
-    return outs
+    outs = pl.pallas_call(
+        hand_on, out_shape=results, in_specs=[anywhere] * 4, out_specs=[anywhere] * 4,
+        scratch_shapes=[pltpu.VMEM(r.shape, r.dtype) for r in results] + [pltpu.SemaphoreType.DMA((2, 4))],
+        name="hand_on",
+    )(*outs)
+    return outs[0].reshape(tokens.shape), outs[1].reshape(tokens.shape), outs[2], outs[3]
 
 
 def solution(mesh):

time: 147 us -> 137 us (0.932)
  local copies, waits for them, and re-layouts: 8.74 us -> 0 us
  other arithmetic: 1.5 us -> 0 us
    unnamed x7 -> x0, local copies, waits for them, and re-layouts: 7.43 us -> none
    pallas_call x1 -> x2, Pallas kernels: 136 us -> 136 us  [the longest x1 133 us: local(): pl.pallas_call(body, out_shape=results, in_specs=[anywhere] * 6, out_spec...]
where the time goes in v3:
time: 137 us; the launch traced here: 136 us
  Pallas kernels  136 us (99%)
    pallas_call x1, Pallas kernels, local(): pl.pallas_call(body, out_shape=results, in_specs=[anywhere] * 6, out_spec...  133 us
    pallas_call x1, Pallas kernels, local(): pl.pallas_call(hand_on, out_shape=results, in_specs=[anywhere] * 4, out_s...  2.95 us

profile of v3, /device:TPU:0, one launch (start us, length us, event | category | flops | bytes accessed | tf_op | source)
XLA Modules:
  0.0 136.4 jit_solution(7191750761828534273)
XLA Ops:
  0.6 132.8 %layer.1 = (bf16[4,16,1536]{2,1,0:T(8,128)(2,1)}, bf16[4,16,1536]{2,1,0:T(8,128)(2,1)}, bf16[1,36,128,128]{3,2,1,0:T(8,128)(2,1)}, bf16[1,36,128,128]{3,2,1,0:T(8,128)(2,1)}) custom-call(s32[2,36]{1,0:T(2,128)} %bitcast.12, s32[2,36]{1,0:T(2,128)} %bitcast.13, bf16[4,16,1536]{2,1,0:T(8,128)(2,1)} %bitcast.10, bf16[4,16,1536]{2,1,0:T(8,128)(2,1)} %bitcast.11, ...), custom_call_target="tpu_custom_call" | custom-call | tf_op jit(solution)/shard_map/layer/pallas_call | solution.py:496
  133.5 3.0 %hand_on.1 = (bf16[4,16,1536]{2,1,0:T(8,128)(2,1)}, bf16[4,16,1536]{2,1,0:T(8,128)(2,1)}, bf16[1,36,128,128]{3,2,1,0:T(8,128)(2,1)}, bf16[1,36,128,128]{3,2,1,0:T(8,128)(2,1)}) custom-call(bf16[4,16,1536]{2,1,0:T(8,128)(2,1)} %get-tuple-element.12.refs_0_, bf16[4,16,1536]{2,1,0:T(8,128)(2,1)} %get-tuple-element.13.refs_1_, ...), custom_call_target="tpu_custom_call" | custom-call | tf_op jit(solution)/shard_map/hand_on/pallas_call | solution.py:537

commit v4 on v3

--- a/solution.py
+++ b/solution.py
@@ -12,12 +12,13 @@
 TILE = 12
 SIDE = BLK * TILE
 CAP = 36
+SLOTS = 12
 TOKENS = 1024
 STAGES = 4
 ROWS = TOKENS // STAGES
 ROW_SHARE = ROWS // 8
 COL_SHARE = ROWS // 16
-WIDE = 512
+WIDE = 768
 CURVE = 0.7978845608028654
 CUBIC = 0.044715
 PLAIN = (((1,), (0,)), ((), ()))
@@ -26,30 +27,30 @@
 COL_GATHER, CORE_GATHER, ROW_SUM, ROW_GATHER, CORE_SUM, COL_SUM, COPIES = 0, 7, 8, 18, 26, 27, 34
 
 
-NEAR = ((0, 0), (0, 1), (2, 0))
-WIDE_FIRST = ((0, 0), (0, 1), (1, 0))
+NEAR = ((1, 0), (1, 1), (3, 0))
+WIDE_FIRST = ((0, 1), (1, 0), (2, 0))
 STEPS = (
-    "gather", "assemble", "gather_mid", "gather_pass", "gather_core", "rise", "sumb_two", "sum_mid", "sumb_one",
-    "sumb_mid", "sum_pair", "sumb_end", "sum_end", "sprb_mid", "flip", "sprb_pass", "spread_mid", "sprb_end", "fall",
-    "spread_pass", "core_end", "out_mid", "spread_end", "out_pair", "slot", "out_end", "pick",
+    "gather", "assemble", "gather_mid", "gather_pass", "gather_core", "rise", "sum_mid", "sum_pair", "sumb_two",
+    "sumb_one", "sum_end", "sumb_mid", "sumb_end", "spread_mid", "sprb_mid", "sprb_pass", "spread_pass", "flip",
+    "sprb_end", "fall", "spread_end", "core_end", "out_mid", "out_pair", "slot", "out_end",
 )
 ORDER = (
-    (0, 0, 0), (0, 1, 0), (1, 0, 0), (0, 2, 0), (2, 0, 0), (2, 1, 0), (2, 2, 0), (0, 3, 0), (3, 0, 0), (3, 1, 0),
-    (2, 3, 0), (3, 2, 0), (0, 0, 1), (1, 0, 1), (4, 0, 0), (0, 1, 1), (4, 1, 0), (3, 3, 0), (5, 0, 0), (4, 2, 0),
-    (5, 1, 0), (4, 3, 0), (0, 2, 1), (0, 3, 1), (5, 2, 0), (6, 0, 0), (2, 1, 1), (7, 1, 0), (2, 0, 1), (5, 3, 0),
-    (3, 0, 1), (8, 0, 0), (3, 1, 1), (9, 0, 0), (10, 1, 0), (2, 2, 1), (4, 0, 1), (7, 3, 0), (3, 2, 1), (6, 2, 0),
-    (2, 3, 1), (5, 0, 1), (4, 2, 1), (8, 2, 0), (11, 0, 0), (10, 3, 0), (9, 2, 0), (5, 2, 1), (12, 1, 0), (13, 0, 0),
-    (3, 3, 1), (11, 2, 0), (14, 0, 1), (6, 0, 1), (4, 3, 1), (7, 2, 1), (4, 1, 1), (14, 3, 0), (8, 0, 1), (5, 3, 1),
-    (13, 1, 0), (5, 1, 1), (14, 1, 1), (12, 3, 0), (9, 0, 1), (14, 1, 0), (10, 2, 1), (14, 3, 1), (14, 0, 0),
-    (14, 2, 0), (14, 2, 1), (7, 3, 1), (15, 0, 0), (16, 2, 0), (15, 1, 0), (7, 1, 1), (16, 3, 0), (11, 0, 1),
-    (12, 2, 1), (10, 3, 1), (17, 0, 0), (18, 0, 0), (19, 2, 0), (17, 1, 0), (18, 1, 0), (10, 1, 1), (20, 0, 0),
-    (19, 3, 0), (16, 2, 1), (20, 1, 0), (21, 0, 0), (12, 3, 1), (13, 0, 1), (21, 1, 0), (12, 1, 1), (22, 2, 0),
-    (18, 2, 0), (23, 0, 0), (22, 3, 0), (18, 3, 0), (19, 2, 1), (20, 2, 0), (16, 3, 1), (24, 0, 0), (20, 3, 0),
-    (15, 0, 1), (21, 2, 0), (16, 1, 1), (25, 0, 0), (23, 1, 0), (24, 1, 0), (22, 2, 1), (18, 2, 1), (23, 2, 0),
-    (17, 0, 1), (18, 0, 1), (19, 1, 1), (19, 3, 1), (20, 2, 1), (21, 3, 0), (24, 2, 0), (20, 0, 1), (21, 2, 1),
-    (22, 1, 1), (18, 1, 1), (22, 3, 1), (18, 3, 1), (21, 0, 1), (23, 3, 0), (20, 1, 1), (23, 2, 1), (26, 0, 0),
-    (20, 3, 1), (24, 0, 1), (25, 3, 0), (21, 1, 1), (21, 3, 1), (25, 1, 0), (23, 0, 1), (24, 1, 1), (23, 1, 1),
-    (23, 3, 1), (24, 2, 1), (25, 0, 1), (25, 2, 0), (25, 2, 1), (25, 1, 1), (26, 0, 1), (25, 3, 1),
+    (0, 0, 0), (0, 1, 0), (1, 0, 0), (0, 2, 0), (2, 0, 0), (2, 1, 0), (2, 2, 0), (3, 0, 0), (3, 1, 0), (3, 2, 0),
+    (4, 0, 0), (0, 3, 0), (0, 0, 1), (1, 0, 1), (0, 3, 1), (0, 2, 1), (4, 1, 0), (5, 0, 0), (2, 3, 0), (4, 2, 0),
+    (2, 0, 1), (0, 1, 1), (5, 1, 0), (3, 3, 0), (6, 0, 0), (2, 1, 1), (3, 0, 1), (5, 2, 0), (4, 3, 0), (2, 2, 1),
+    (3, 1, 1), (7, 0, 0), (5, 3, 0), (4, 0, 1), (8, 1, 0), (9, 1, 0), (4, 1, 1), (6, 2, 0), (5, 0, 1), (7, 2, 0),
+    (2, 3, 1), (10, 0, 0), (11, 1, 0), (8, 3, 0), (6, 0, 1), (3, 3, 1), (5, 1, 1), (3, 2, 1), (12, 1, 0), (9, 3, 0),
+    (10, 2, 0), (13, 0, 0), (4, 2, 1), (5, 2, 1), (14, 1, 0), (8, 1, 1), (7, 0, 1), (9, 1, 1), (15, 1, 0), (16, 0, 0),
+    (14, 2, 0), (6, 2, 1), (11, 1, 1), (11, 3, 0), (4, 3, 1), (5, 3, 1), (12, 3, 0), (15, 2, 0), (17, 0, 1),
+    (18, 1, 0), (19, 1, 0), (7, 2, 1), (10, 0, 1), (6, 3, 1), (13, 3, 0), (12, 1, 1), (18, 2, 0), (19, 2, 0),
+    (17, 1, 1), (14, 0, 1), (17, 3, 0), (20, 0, 0), (19, 0, 0), (10, 2, 1), (16, 3, 0), (7, 3, 1), (21, 2, 0),
+    (17, 3, 1), (21, 1, 0), (13, 1, 1), (15, 0, 1), (17, 0, 0), (13, 2, 1), (20, 3, 0), (19, 3, 0), (22, 2, 0),
+    (10, 3, 1), (22, 1, 0), (21, 0, 0), (16, 1, 1), (18, 0, 1), (19, 0, 1), (21, 3, 0), (13, 3, 1), (17, 2, 1),
+    (21, 0, 1), (16, 2, 1), (20, 1, 1), (19, 1, 1), (23, 2, 0), (22, 0, 0), (22, 3, 0), (16, 3, 1), (24, 2, 0),
+    (22, 0, 1), (20, 2, 1), (19, 2, 1), (21, 1, 1), (23, 0, 0), (20, 3, 1), (19, 3, 1), (21, 2, 1), (22, 1, 1),
+    (23, 0, 1), (23, 1, 0), (17, 1, 0), (23, 3, 0), (21, 3, 1), (24, 1, 0), (17, 2, 0), (22, 2, 1), (23, 1, 1),
+    (24, 2, 1), (22, 3, 1), (24, 0, 1), (25, 0, 0), (25, 3, 0), (25, 1, 1), (25, 2, 0), (23, 2, 1), (23, 3, 1),
+    (25, 1, 0), (24, 1, 1), (25, 0, 1), (24, 0, 0), (25, 2, 1), (25, 3, 1),
 )
 
 
@@ -57,7 +58,7 @@
     widen_at, narrow_at, tokens, cotangent, widen_blocks, narrow_blocks,
     layer_output, token_grad, widen_grad, narrow_grad,
     gathered, terms, fields, tiles, row_one, row_two, row_pair, row_send, core_in,
-    col_one, col_two, col_pair, col_send, hidden, widen_spare, narrow_spare, flipped, dense, picked, results, at, marks, places,
+    col_one, col_two, col_pair, col_send, hidden, widen_spare, narrow_spare, flipped, blocked, at, marks, places,
     send_sem, recv_sem, here_sem,
 ):
     row, col = lax.axis_index("row"), lax.axis_index("col")
@@ -93,21 +94,10 @@
     for partner in partners:
         pl.semaphore_signal(barrier, inc=1, device_id=partner, device_id_type=MESH)
 
-    def place(a, i):
-        return (at[a, 0, i] + 1) * TILE + at[a, 1, i] + 1
-
-    count = lax.broadcasted_iota(jnp.int32, (1, 2 * BLK), 1)
-    for a in range(2):
-        loads[1 + a].wait()
-        marks[a:a + 1] = lax.fori_loop(
-            0, CAP, lambda i, mark: jnp.where(count == place(a, i), i, mark), jnp.full((1, 2 * BLK), CAP, jnp.int32)
-        )
-    loads[6] = pltpu.make_async_copy(marks, places, here_sem.at[6])
-    loads[6].start()
     for a in range(2):
         spare[a][CAP] = jnp.zeros((BLK, BLK), jnp.bfloat16)
-    dense[0] = jnp.zeros((BLK, BLK), jnp.bfloat16)
-    loads[6].wait()
+        flipped[a, 0] = jnp.zeros((BLK, TOKENS), jnp.bfloat16)
+        blocked[a, :, 0] = jnp.zeros((STAGES, ROWS, BLK), jnp.bfloat16)
     pl.semaphore_wait(barrier, len(partners))
 
     copies = {}
@@ -274,18 +264,33 @@
 
     row_ring = Ring(z, y_lo, ROW_SHARE, 0, z_next, z_back, y_near)
     col_ring = Ring(x, y_hi, COL_SHARE, core * (ROWS // 2), x_next, x_back, y_far)
-    outputs, stores = (layer_output, token_grad), []
+    outputs = (layer_output, token_grad)
 
     def product(source, tile, dims, target):
-        @pl.loop(0, SIDE // WIDE)
-        def _(j):
-            part = pl.ds(pl.multiple_of(j * WIDE, WIDE), WIDE)
+        for j in range(SIDE // WIDE):
+            part = pl.ds(j * WIDE, WIDE)
             other = tiles[tile, :, part] if dims is PLAIN else tiles[tile, part, :]
             target[:, part] = lax.dot_general(
                 source[...], other, dims, preferred_element_type=jnp.float32
             ).astype(jnp.bfloat16)
 
+    def find_places():
+        count = lax.broadcasted_iota(jnp.int32, (1, 2 * BLK), 1)
+        for a in range(2):
+            loads[1 + a].wait()
+
+            def mark(i, found):
+                return jnp.where(count == (at[a, 0, i] + 1) * TILE + at[a, 1, i] + 1, i, found)
+
+            marks[a:a + 1] = lax.fori_loop(0, CAP, mark, jnp.full((1, 2 * BLK), CAP, jnp.int32), unroll=6)
+        load = pltpu.make_async_copy(marks, places, here_sem.at[6])
+        load.start()
+        load.wait()
+
     def assemble(s, a):
+        if 1 in loads:
+            find_places()
+            del loads[1]
         loads[4 + a].wait()
 
         @pl.loop(0, TILE)
@@ -296,8 +301,8 @@
                 ]
 
     def gather(s, a):
-        if s == 0:
-            loads[3 * a].wait()
+        if 3 * a in loads:
+            loads.pop(3 * a).wait()
         col_ring.spread(gathered, s, a, COL_GATHER)
 
     def gather_mid(s, a):
@@ -387,6 +392,8 @@
         for k in range(ROW_SUM, ROW_GATHER):
             if (s, a, k) in copies:
                 copies.pop((s, a, k)).wait_send()
+        for c in range(TILE):
+            blocked[a, s, c + 1] = fields[a, s, :, c * BLK:(c + 1) * BLK]
         product(fields.at[a, s], 1 - a, (PLAIN, FLIPPED)[a], terms.at[a, s])
         half = span(terms, a, s, (1 - core) * (ROWS // 2), ROWS // 2)
         send(s, a, CORE_SUM, half, core_in.at[a, s], other_core)
@@ -405,57 +412,30 @@
 
     def out_end(s, a):
         refs = col_ring.total_end(terms, col_two, col_pair, s, a, COL_SUM)
-        add_into(results.at[a, s], refs, COL_SHARE)
-        store = pltpu.make_async_copy(results.at[a, s], outputs[a].at[s], here_sem.at[9 + a * STAGES + s])
-        store.start()
-        stores.append(store)
+        add_into(outputs[a].at[s], refs, COL_SHARE)
 
     def flip(s, a):
         source = gathered.at[a, s]
 
-        @pl.loop(0, TILE)
-        def _(i):
-            part = pl.ds(pl.multiple_of(i * BLK, BLK), BLK)
-            flipped[a, part, s * ROWS:(s + 1) * ROWS] = source[:, part].T
+        for i in range(TILE):
+            flipped[a, i + 1, :, s * ROWS:(s + 1) * ROWS] = source[:, i * BLK:(i + 1) * BLK].T
 
     def slot(j, a):
-        part = pl.ds(j * WIDE, WIDE)
-        right = fields[a, :, :, part].reshape(TOKENS, WIDE)
-
-        @pl.loop(0, SIDE // WIDE)
-        def _(i):
+        for i in range(j * SLOTS, (j + 1) * SLOTS):
+            r, c = at[1 - a, 0, i] + 1, at[1 - a, 1, i] + 1
+            left, right = (c, r) if a == 0 else (r, c)
             value = lax.dot_general(
-                flipped[1 - a, pl.ds(pl.multiple_of(i * WIDE, WIDE), WIDE), :], right, PLAIN,
+                flipped[1 - a, left], blocked[a, :, right].reshape(TOKENS, BLK), PLAIN,
                 preferred_element_type=jnp.float32,
             )
             value = (value * (1.0 / 32.0)).astype(jnp.bfloat16)
-            for r in range(WIDE // BLK):
-                for c in range(WIDE // BLK):
-                    spot = (i * (WIDE // BLK) + r + 1) * TILE + j * (WIDE // BLK) + c + 1
-                    dense[spot] = value[r * BLK:(r + 1) * BLK, c * BLK:(c + 1) * BLK]
-
-    def pick(s, a):
-        target = (narrow_grad, widen_grad)[a]
-
-        @pl.loop(0, CAP // 4)
-        def _(g):
-            for u in range(4):
-                i = g * 4 + u
-                if a == 0:
-                    row_at, col_at = at[1, 0, i], at[1, 1, i]
-                    picked[a, i] = dense[(col_at + 1) * TILE + row_at + 1].T
-                else:
-                    picked[a, i] = dense[place(0, i)]
-
-        store = pltpu.make_async_copy(picked.at[a], target.at[0], here_sem.at[7 + a])
-        store.start()
-        stores.append(store)
+            (narrow_grad, widen_grad)[a][0, i] = value.T if a == 0 else value
 
     steps = {
         step.__name__: step
         for step in (
             assemble, gather, gather_mid, gather_pass, gather_core, rise, sum_mid, sum_pair, sum_end, spread_mid,
-            spread_pass, spread_end, fall, core_end, out_mid, out_pair, out_end, flip, slot, pick,
+            spread_pass, spread_end, fall, core_end, out_mid, out_pair, out_end, flip, slot,
             sumb_two, sumb_one, sumb_mid, sumb_end, sprb_mid, sprb_pass, sprb_end,
         )
     }
@@ -463,26 +443,25 @@
         steps[STEPS[index]](s, a)
     for copy in copies.values():
         copy.wait_send()
+
+
+def hand_on(*refs):
+    sources, targets, sem = refs[:4], refs[4:8], refs[8]
+    stores = []
+    for i in range(4):
+        for j in range(1 if i < 2 else CAP // SLOTS):
+            part = pl.ds(j * SLOTS, SLOTS)
+            source = sources[i] if i < 2 else sources[i].at[0, part]
+            target = targets[i] if i < 2 else targets[i].at[0, part]
+            stores.append(pltpu.make_async_copy(source, target, sem.at[i, j]))
+            stores[-1].start()
     for store in stores:
         store.wait()
 
 
-def hand_on(*refs):
-    sources, targets, rooms, sem = refs[:4], refs[4:8], refs[8:12], refs[12]
-    loads = [pltpu.make_async_copy(a, b, sem.at[0, i]) for i, (a, b) in enumerate(zip(sources, rooms))]
-    stores = [pltpu.make_async_copy(a, b, sem.at[1, i]) for i, (a, b) in enumerate(zip(rooms, targets))]
-    for load in loads:
-        load.start()
-    for load, store in zip(loads, stores):
-        load.wait()
-        store.start()
-    for store in stores:
-        store.wait()
-
-
 def local(tokens, widen_blocks, widen_pattern, narrow_blocks, narrow_pattern, cotangent):
     grouped = (STAGES, COL_SHARE, SIDE)
-    anywhere = pl.BlockSpec(memory_space=pl.ANY)
+    anywhere, vmem = pl.BlockSpec(memory_space=pl.ANY), pl.BlockSpec(memory_space=pltpu.VMEM)
     results = (
         jax.ShapeDtypeStruct(grouped, jnp.bfloat16),
         jax.ShapeDtypeStruct(grouped, jnp.bfloat16),
@@ -495,9 +474,9 @@
 
     outs = pl.pallas_call(
         body,
-        out_shape=results,
+        out_shape=tuple(pltpu.VMEM(r.shape, r.dtype) for r in results),
         in_specs=[anywhere] * 6,
-        out_specs=[anywhere] * 4,
+        out_specs=[vmem] * 4,
         scratch_shapes=[
             room(2, STAGES, ROWS),
             room(2, STAGES, ROWS),
@@ -515,19 +494,17 @@
             room(STAGES, ROW_SHARE, dtype=jnp.float32),
             pltpu.VMEM((CAP + 1, BLK, BLK), jnp.bfloat16),
             pltpu.VMEM((CAP + 1, BLK, BLK), jnp.bfloat16),
-            pltpu.VMEM((2, SIDE, TOKENS), jnp.bfloat16),
-            pltpu.VMEM((TILE * (TILE + 1) + 1, BLK, BLK), jnp.bfloat16),
-            pltpu.VMEM((2, CAP, BLK, BLK), jnp.bfloat16),
-            pltpu.VMEM((2, *grouped), jnp.bfloat16),
+            pltpu.VMEM((2, TILE + 1, BLK, TOKENS), jnp.bfloat16),
+            pltpu.VMEM((2, STAGES, TILE + 1, ROWS, BLK), jnp.bfloat16),
             pltpu.SMEM((2, 2, CAP), jnp.int32),
             pltpu.VMEM((2, 2 * BLK), jnp.int32),
             pltpu.SMEM((2, 2 * BLK), jnp.int32),
             pltpu.SemaphoreType.DMA((2, STAGES, COPIES)),
             pltpu.SemaphoreType.DMA((2, STAGES, COPIES)),
-            pltpu.SemaphoreType.DMA((9 + 2 * STAGES,)),
+            pltpu.SemaphoreType.DMA((7,)),
         ],
         compiler_params=pltpu.CompilerParams(
-            collective_id=0, has_side_effects=True, vmem_limit_bytes=62 * 2**20
+            collective_id=0, has_side_effects=True, vmem_limit_bytes=57 * 2**20
         ),
         name="layer",
     )(
@@ -535,10 +512,9 @@
         widen_blocks, narrow_blocks,
     )
     outs = pl.pallas_call(
-        hand_on, out_shape=results, in_specs=[anywhere] * 4, out_specs=[anywhere] * 4,
-        scratch_shapes=[pltpu.VMEM(r.shape, r.dtype) for r in results] + [pltpu.SemaphoreType.DMA((2, 4))],
-        name="hand_on",
-    )(*outs)
+        hand_on, out_shape=results, in_specs=[vmem] * 4, out_specs=[anywhere] * 4,
+        scratch_shapes=[pltpu.SemaphoreType.DMA((4, CAP // SLOTS))], name="hand_on",
+    )(*(pltpu.with_memory_space_constraint(o, pltpu.VMEM) for o in outs))
     return outs[0].reshape(tokens.shape), outs[1].reshape(tokens.shape), outs[2], outs[3]
 
 

time: 137 us -> 132 us (0.964)
  Pallas kernels: 136 us -> 131 us
    pallas_call x2, Pallas kernels: 136 us -> 131 us  [the longest x1 130 us: local(): pl.pallas_call(body, out_shape=tuple((pltpu.VMEM(r.shape, r.dtype) for r...]
where the time goes in v4:
time: 132 us
  Pallas kernels  131 us (99%)
    pallas_call x1, Pallas kernels, local(): pl.pallas_call(body, out_shape=tuple((pltpu.VMEM(r.shape, r.dtype) for r...  130 us

profile of v4, /device:TPU:0, one launch (start us, length us, event | category | flops | bytes accessed | tf_op | source)
XLA Modules:
  0.0 132.1 jit_solution(2661661569369926804)
XLA Ops:
  0.6 129.6 %layer.1 = (bf16[4,16,1536]{2,1,0:T(8,128)(2,1)S(1)}, bf16[4,16,1536]{2,1,0:T(8,128)(2,1)S(1)}, bf16[1,36,128,128]{3,2,1,0:T(8,128)(2,1)S(1)}, bf16[1,36,128,128]{3,2,1,0:T(8,128)(2,1)S(1)}) custom-call(s32[2,36]{1,0:T(2,128)} %bitcast.12, s32[2,36]{1,0:T(2,128)} %bitcast.13, bf16[4,16,1536]{2,1,0:T(8,128)(2,1)} %bitcast.10, bf16[4,16,1536]{2,1,0:T(8,128)(2,1)} %bitcast.11, ...), custom_call_target="tpu_custom_call" | custom-call | tf_op jit(solution)/shard_map/layer/pallas_call | solution.py:475
  130.3 1.6 %hand_on.1 = (bf16[4,16,1536]{2,1,0:T(8,128)(2,1)}, bf16[4,16,1536]{2,1,0:T(8,128)(2,1)}, bf16[1,36,128,128]{3,2,1,0:T(8,128)(2,1)}, bf16[1,36,128,128]{3,2,1,0:T(8,128)(2,1)}) custom-call(bf16[4,16,1536]{2,1,0:T(8,128)(2,1)S(1)} %get-tuple-element.12.refs_0_, bf16[4,16,1536]{2,1,0:T(8,128)(2,1)S(1)} %get-tuple-element.13.refs_1_, ...), custom_call_target="tpu_custom_call" | custom-call | tf_op jit(solution)/shard_map/hand_on/pallas_call | solution.py:514

commit v5 on v4

--- a/solution.py
+++ b/solution.py
@@ -27,30 +27,30 @@
 COL_GATHER, CORE_GATHER, ROW_SUM, ROW_GATHER, CORE_SUM, COL_SUM, COPIES = 0, 7, 8, 18, 26, 27, 34
 
 
-NEAR = ((1, 0), (1, 1), (3, 0))
-WIDE_FIRST = ((0, 1), (1, 0), (2, 0))
+NEAR = ((0, 1), (2, 0), (2, 1), (3, 0))
+WIDE_FIRST = ((1, 1), (2, 1), (3, 1))
 STEPS = (
-    "gather", "assemble", "gather_mid", "gather_pass", "gather_core", "rise", "sum_mid", "sum_pair", "sumb_two",
-    "sumb_one", "sum_end", "sumb_mid", "sumb_end", "spread_mid", "sprb_mid", "sprb_pass", "spread_pass", "flip",
-    "sprb_end", "fall", "spread_end", "core_end", "out_mid", "out_pair", "slot", "out_end",
+    "gather", "assemble", "gather_mid", "gather_pass", "gather_core", "rise", "sum_mid", "sum_pair", "sum_end",
+    "flip", "sumb_two", "sumb_one", "spread_mid", "sumb_mid", "spread_pass", "sumb_end", "spread_end", "fall",
+    "core_end", "sprb_mid", "sprb_pass", "out_mid", "sprb_end", "out_pair", "slot", "out_end",
 )
 ORDER = (
-    (0, 0, 0), (0, 1, 0), (1, 0, 0), (0, 2, 0), (2, 0, 0), (2, 1, 0), (2, 2, 0), (3, 0, 0), (3, 1, 0), (3, 2, 0),
-    (4, 0, 0), (0, 3, 0), (0, 0, 1), (1, 0, 1), (0, 3, 1), (0, 2, 1), (4, 1, 0), (5, 0, 0), (2, 3, 0), (4, 2, 0),
-    (2, 0, 1), (0, 1, 1), (5, 1, 0), (3, 3, 0), (6, 0, 0), (2, 1, 1), (3, 0, 1), (5, 2, 0), (4, 3, 0), (2, 2, 1),
-    (3, 1, 1), (7, 0, 0), (5, 3, 0), (4, 0, 1), (8, 1, 0), (9, 1, 0), (4, 1, 1), (6, 2, 0), (5, 0, 1), (7, 2, 0),
-    (2, 3, 1), (10, 0, 0), (11, 1, 0), (8, 3, 0), (6, 0, 1), (3, 3, 1), (5, 1, 1), (3, 2, 1), (12, 1, 0), (9, 3, 0),
-    (10, 2, 0), (13, 0, 0), (4, 2, 1), (5, 2, 1), (14, 1, 0), (8, 1, 1), (7, 0, 1), (9, 1, 1), (15, 1, 0), (16, 0, 0),
-    (14, 2, 0), (6, 2, 1), (11, 1, 1), (11, 3, 0), (4, 3, 1), (5, 3, 1), (12, 3, 0), (15, 2, 0), (17, 0, 1),
-    (18, 1, 0), (19, 1, 0), (7, 2, 1), (10, 0, 1), (6, 3, 1), (13, 3, 0), (12, 1, 1), (18, 2, 0), (19, 2, 0),
-    (17, 1, 1), (14, 0, 1), (17, 3, 0), (20, 0, 0), (19, 0, 0), (10, 2, 1), (16, 3, 0), (7, 3, 1), (21, 2, 0),
-    (17, 3, 1), (21, 1, 0), (13, 1, 1), (15, 0, 1), (17, 0, 0), (13, 2, 1), (20, 3, 0), (19, 3, 0), (22, 2, 0),
-    (10, 3, 1), (22, 1, 0), (21, 0, 0), (16, 1, 1), (18, 0, 1), (19, 0, 1), (21, 3, 0), (13, 3, 1), (17, 2, 1),
-    (21, 0, 1), (16, 2, 1), (20, 1, 1), (19, 1, 1), (23, 2, 0), (22, 0, 0), (22, 3, 0), (16, 3, 1), (24, 2, 0),
-    (22, 0, 1), (20, 2, 1), (19, 2, 1), (21, 1, 1), (23, 0, 0), (20, 3, 1), (19, 3, 1), (21, 2, 1), (22, 1, 1),
-    (23, 0, 1), (23, 1, 0), (17, 1, 0), (23, 3, 0), (21, 3, 1), (24, 1, 0), (17, 2, 0), (22, 2, 1), (23, 1, 1),
-    (24, 2, 1), (22, 3, 1), (24, 0, 1), (25, 0, 0), (25, 3, 0), (25, 1, 1), (25, 2, 0), (23, 2, 1), (23, 3, 1),
-    (25, 1, 0), (24, 1, 1), (25, 0, 1), (24, 0, 0), (25, 2, 1), (25, 3, 1),
+    (0, 0, 0), (0, 0, 1), (1, 0, 0), (0, 1, 0), (2, 0, 0), (2, 0, 1), (2, 1, 0), (3, 0, 0), (1, 0, 1), (3, 0, 1),
+    (3, 1, 0), (0, 2, 1), (0, 1, 1), (0, 3, 0), (4, 0, 0), (5, 0, 0), (2, 1, 1), (4, 0, 1), (0, 2, 0), (4, 1, 0),
+    (0, 3, 1), (2, 3, 0), (2, 2, 1), (5, 0, 1), (3, 1, 1), (6, 0, 0), (5, 1, 0), (3, 2, 1), (7, 0, 0), (4, 1, 1),
+    (2, 2, 0), (6, 1, 0), (5, 1, 1), (2, 3, 1), (4, 2, 1), (7, 1, 0), (8, 0, 0), (6, 1, 1), (5, 2, 1), (9, 1, 1),
+    (10, 0, 1), (11, 0, 1), (8, 1, 0), (12, 0, 0), (3, 2, 0), (3, 3, 0), (7, 1, 1), (9, 0, 1), (3, 3, 1), (10, 2, 1),
+    (4, 2, 0), (5, 2, 0), (13, 0, 1), (14, 0, 0), (4, 3, 1), (4, 3, 0), (11, 2, 1), (15, 0, 1), (5, 3, 1), (12, 1, 0),
+    (8, 1, 1), (16, 0, 0), (9, 3, 1), (5, 3, 0), (10, 2, 0), (11, 2, 0), (14, 1, 0), (17, 0, 0), (13, 2, 1),
+    (13, 2, 0), (18, 0, 0), (10, 3, 0), (19, 1, 1), (6, 3, 1), (15, 2, 0), (16, 1, 0), (17, 1, 0), (9, 2, 0),
+    (20, 1, 1), (18, 1, 0), (12, 0, 1), (15, 2, 1), (21, 1, 0), (14, 0, 1), (7, 3, 1), (9, 3, 0), (12, 2, 0),
+    (21, 0, 0), (22, 1, 1), (11, 3, 0), (13, 3, 0), (19, 2, 1), (17, 1, 1), (16, 0, 1), (14, 2, 0), (17, 0, 1),
+    (9, 0, 0), (15, 3, 0), (20, 2, 1), (8, 3, 1), (18, 0, 1), (18, 1, 1), (9, 1, 0), (16, 2, 0), (17, 2, 0),
+    (12, 3, 0), (18, 2, 0), (19, 3, 1), (22, 2, 1), (17, 2, 1), (21, 1, 1), (14, 3, 0), (9, 2, 1), (20, 3, 1),
+    (21, 0, 1), (23, 1, 0), (18, 2, 1), (23, 0, 0), (16, 3, 0), (21, 2, 0), (17, 3, 0), (21, 2, 1), (22, 3, 1),
+    (17, 3, 1), (18, 3, 0), (24, 0, 0), (23, 0, 1), (18, 3, 1), (23, 2, 0), (23, 2, 1), (23, 1, 1), (24, 1, 0),
+    (21, 3, 0), (24, 0, 1), (21, 3, 1), (25, 1, 0), (24, 2, 0), (23, 3, 0), (25, 0, 0), (25, 0, 1), (23, 3, 1),
+    (25, 2, 0), (25, 2, 1), (24, 1, 1), (24, 2, 1), (25, 1, 1), (25, 3, 0), (25, 3, 1),
 )
 
 

time: 132 us -> 129 us (0.977)
  Pallas kernels: 131 us -> 128 us
    pallas_call x1, Pallas kernels: 130 us -> 126 us  [local(): pl.pallas_call(body, out_shape=tuple((pltpu.VMEM(r.shape, r.dtype) for r...]
where the time goes in v5:
time: 129 us
  Pallas kernels  128 us (99%)
    pallas_call x1, Pallas kernels, local(): pl.pallas_call(body, out_shape=tuple((pltpu.VMEM(r.shape, r.dtype) for r...  126 us

profile of v5, /device:TPU:0, one launch (start us, length us, event | category | flops | bytes accessed | tf_op | source)
XLA Modules:
  0.0 128.5 jit_solution(1275424165137112333)
XLA Ops:
  0.6 126.1 %layer.1 = (bf16[4,16,1536]{2,1,0:T(8,128)(2,1)S(1)}, bf16[4,16,1536]{2,1,0:T(8,128)(2,1)S(1)}, bf16[1,36,128,128]{3,2,1,0:T(8,128)(2,1)S(1)}, bf16[1,36,128,128]{3,2,1,0:T(8,128)(2,1)S(1)}) custom-call(s32[2,36]{1,0:T(2,128)} %bitcast.12, s32[2,36]{1,0:T(2,128)} %bitcast.13, bf16[4,16,1536]{2,1,0:T(8,128)(2,1)} %bitcast.10, bf16[4,16,1536]{2,1,0:T(8,128)(2,1)} %bitcast.11, ...), custom_call_target="tpu_custom_call" | custom-call | tf_op jit(solution)/shard_map/layer/pallas_call | solution.py:475
  126.7 1.6 %hand_on.1 = (bf16[4,16,1536]{2,1,0:T(8,128)(2,1)}, bf16[4,16,1536]{2,1,0:T(8,128)(2,1)}, bf16[1,36,128,128]{3,2,1,0:T(8,128)(2,1)}, bf16[1,36,128,128]{3,2,1,0:T(8,128)(2,1)}) custom-call(bf16[4,16,1536]{2,1,0:T(8,128)(2,1)S(1)} %get-tuple-element.12.refs_0_, bf16[4,16,1536]{2,1,0:T(8,128)(2,1)S(1)} %get-tuple-element.13.refs_1_, ...), custom_call_target="tpu_custom_call" | custom-call | tf_op jit(solution)/shard_map/hand_on/pallas_call | solution.py:514

commit v6 on v5

--- a/solution.py
+++ b/solution.py
@@ -392,11 +392,18 @@
         for k in range(ROW_SUM, ROW_GATHER):
             if (s, a, k) in copies:
                 copies.pop((s, a, k)).wait_send()
+        near, far = core * (ROWS // 2), (1 - core) * (ROWS // 2)
+        half = span(terms, a, s, far, ROWS // 2)
+        dims = (PLAIN, FLIPPED)[a]
+        if s == STAGES - 1:
+            product(span(fields, a, s, far, ROWS // 2), 1 - a, dims, half)
+            send(s, a, CORE_SUM, half, core_in.at[a, s], other_core)
+            product(span(fields, a, s, near, ROWS // 2), 1 - a, dims, span(terms, a, s, near, ROWS // 2))
+        else:
+            product(fields.at[a, s], 1 - a, dims, terms.at[a, s])
+            send(s, a, CORE_SUM, half, core_in.at[a, s], other_core)
         for c in range(TILE):
             blocked[a, s, c + 1] = fields[a, s, :, c * BLK:(c + 1) * BLK]
-        product(fields.at[a, s], 1 - a, (PLAIN, FLIPPED)[a], terms.at[a, s])
-        half = span(terms, a, s, (1 - core) * (ROWS // 2), ROWS // 2)
-        send(s, a, CORE_SUM, half, core_in.at[a, s], other_core)
 
     def core_end(s, a):
         arrived(s, a, CORE_SUM)

time: 129 us -> 131 us (1.016)
  Pallas kernels: 128 us -> 130 us
    pallas_call x1, Pallas kernels: 126 us -> 129 us  [local(): pl.pallas_call(body, out_shape=tuple((pltpu.VMEM(r.shape, r.dtype) for r...]
where the time goes in v6:
time: 131 us
  Pallas kernels  130 us (99%)
    pallas_call x1, Pallas kernels, local(): pl.pallas_call(body, out_shape=tuple((pltpu.VMEM(r.shape, r.dtype) for r...  129 us

profile of v6, /device:TPU:0, one launch (start us, length us, event | category | flops | bytes accessed | tf_op | source)
XLA Modules:
  0.0 131.0 jit_solution(14201632797796502703)
XLA Ops:
  0.6 128.5 %layer.1 = (bf16[4,16,1536]{2,1,0:T(8,128)(2,1)S(1)}, bf16[4,16,1536]{2,1,0:T(8,128)(2,1)S(1)}, bf16[1,36,128,128]{3,2,1,0:T(8,128)(2,1)S(1)}, bf16[1,36,128,128]{3,2,1,0:T(8,128)(2,1)S(1)}) custom-call(s32[2,36]{1,0:T(2,128)} %bitcast.12, s32[2,36]{1,0:T(2,128)} %bitcast.13, bf16[4,16,1536]{2,1,0:T(8,128)(2,1)} %bitcast.10, bf16[4,16,1536]{2,1,0:T(8,128)(2,1)} %bitcast.11, ...), custom_call_target="tpu_custom_call" | custom-call | tf_op jit(solution)/shard_map/layer/pallas_call | solution.py:482
  129.2 1.6 %hand_on.1 = (bf16[4,16,1536]{2,1,0:T(8,128)(2,1)}, bf16[4,16,1536]{2,1,0:T(8,128)(2,1)}, bf16[1,36,128,128]{3,2,1,0:T(8,128)(2,1)}, bf16[1,36,128,128]{3,2,1,0:T(8,128)(2,1)}) custom-call(bf16[4,16,1536]{2,1,0:T(8,128)(2,1)S(1)} %get-tuple-element.12.refs_0_, bf16[4,16,1536]{2,1,0:T(8,128)(2,1)S(1)} %get-tuple-element.13.refs_1_, ...), custom_call_target="tpu_custom_call" | custom-call | tf_op jit(solution)/shard_map/hand_on/pallas_call | solution.py:521
